TPU v7x, 512 devices: a whole 4x4x16 slice. The times are simulated.
512 devices in a mesh: slide: 16 (over z_lo, x), tile: 32 (over y, z_hi, core).
Axes of the slice: x: 4, y: 4, z: 16 (z_hi: 4, z_lo: 4; z = z_hi * 4 + z_lo), core: 2. Of those that a mesh axis runs over, the one named last changes fastest.
Arguments:
- tiles: bfloat16 [32768, 16, 1024], P(('slide', 'tile')), parts along dimension 0, may hold values from -6 to 6
- w_reduce: bfloat16 [1024, 256], replicated, may hold values from -0.1875 to 0.1875
- w_expand: bfloat16 [1024, 256], replicated, may hold values from -0.375 to 0.375
- att_tanh: bfloat16 [1024, 256], replicated, may hold values from -0.1875 to 0.1875
- att_gate: bfloat16 [1024, 256], replicated, may hold values from -0.1875 to 0.1875
- att_vector: float32 [256], replicated, may hold values from -0.3 to 0.3
- classifier: float32 [1024, 2], replicated, may hold values from -0.09375 to 0.09375
- tile_counts: int32 [512], P(('slide', 'tile')), parts along dimension 0, may hold values from 1 to 64, 1024 in all
- target_weights: float32 [32], P('slide'), parts along dimension 0, may hold values from 0.1 to 1
Outputs:
- grad_w1: float32 [16384, 256], P(('slide', 'tile')), parts along dimension 0
- grad_w2: float32 [16384, 256], P(('slide', 'tile')), parts along dimension 0
- loss: float32 [16], P('slide'), parts along dimension 0
There are 16 independent parts, one for each index of `slide`. A program takes and returns all parts, laid end to end along the dimension named above; an argument that names none is the same for every part. Nothing has to cross between parts.
Inputs may be any that keep to these rules, and one draw needn't show every extreme that they name: `tile_counts`: per device tile counts sum to exactly 1024 over a slide, and some device holds exactly 64.
All inputs are finite; a program needn't handle non-finite values.
Results may differ from a plain program's by a relative error of at most 0.008.
Values may be sent and summed in bfloat16 or wider, within the bound.
No kernel may reach another device: no remote copies, remote signals or barrier semaphores. Data moves between devices by JAX's collectives and lax.ppermute only.
A program may use at most 64 MiB of HBM per device.

v0:
```python
import jax
import jax.numpy as jnp
from jax import lax
from jax.sharding import PartitionSpec as P


def attend(embed, att_tanh, att_gate, att_vector):
    tanh_part = jnp.tanh(jnp.dot(embed, att_tanh, preferred_element_type=jnp.float32))
    gate_part = jax.nn.sigmoid(jnp.dot(embed, att_gate, preferred_element_type=jnp.float32))
    score = jnp.sum(tanh_part * gate_part * att_vector, axis=1)
    return (tanh_part, gate_part, score)


def body(
    tiles,
    w_reduce,
    w_expand,
    att_tanh,
    att_gate,
    att_vector,
    classifier,
    tile_counts,
    target_weights,
):
    slots, positions, width = tiles.shape
    live = (jnp.arange(slots, dtype=jnp.int32) < tile_counts[0]).astype(jnp.float32)
    flat = tiles.reshape(slots * positions, width)
    hidden = jnp.maximum(jnp.dot(flat, w_reduce, preferred_element_type=jnp.float32), 0.0).astype(
        jnp.bfloat16
    )
    expanded = lax.dot_general(
        hidden, w_expand, (((1,), (1,)), ((), ())), preferred_element_type=jnp.float32
    )
    output = flat.astype(jnp.float32) + expanded
    embed = (jnp.sum(output.reshape(slots, positions, width), axis=1) / positions).astype(
        jnp.bfloat16
    )
    tanh_part, gate_part, score = attend(embed, att_tanh, att_gate, att_vector)
    weight = live * jnp.exp(score)
    embed_float = embed.astype(jnp.float32)
    piece_embed = lax.all_gather(embed, "tile", axis=0, tiled=True)
    piece_live = lax.all_gather(live.astype(jnp.bfloat16), "tile", axis=0, tiled=True)
    unused_tanh, unused_gate, piece_score = attend(piece_embed, att_tanh, att_gate, att_vector)
    piece_weight = piece_live.astype(jnp.float32) * jnp.exp(piece_score)
    total = jnp.sum(piece_weight)
    numer = jnp.sum(piece_weight[:, None] * piece_embed.astype(jnp.float32), axis=0)
    pooled = numer / total
    target_share = target_weights / jnp.sum(target_weights)
    class_scores = jnp.sum(pooled[:, None] * classifier, axis=0)
    log_partition_sum = jnp.log(jnp.sum(jnp.exp(class_scores)))
    loss = log_partition_sum - jnp.sum(class_scores * target_share)
    slide_tile_count = lax.axis_size("tile") * slots // 2
    logit_gradient = slide_tile_count * (jnp.exp(class_scores - log_partition_sum) - target_share)
    pooled_gradient = jnp.sum(classifier * logit_gradient[None, :], axis=1)
    prob = weight / total
    dscore = prob * (
        jnp.sum(embed_float * pooled_gradient, axis=1) - jnp.sum(pooled * pooled_gradient)
    )
    dact = dscore[:, None] * att_vector
    dtanh = (dact * gate_part * (1.0 - tanh_part * tanh_part)).astype(jnp.bfloat16)
    dgate = (dact * tanh_part * gate_part * (1.0 - gate_part)).astype(jnp.bfloat16)
    back_dims = (((1,), (1,)), ((), ()))
    dembed = prob[:, None] * pooled_gradient + lax.dot_general(
        dtanh, att_tanh, back_dims, preferred_element_type=jnp.float32
    )
    dembed = dembed + lax.dot_general(
        dgate, att_gate, back_dims, preferred_element_type=jnp.float32
    )
    dout = (dembed / positions).astype(jnp.bfloat16)
    spread = jnp.broadcast_to(dout[:, None, :], (slots, positions, width)).reshape(
        slots * positions, width
    )
    row_dims = (((0,), (0,)), ((), ()))
    dhid = jnp.dot(spread, w_expand, preferred_element_type=jnp.float32)
    dhid = (dhid * (hidden > 0).astype(jnp.float32)).astype(jnp.bfloat16)
    local_w1 = lax.dot_general(flat, dhid, row_dims, preferred_element_type=jnp.float32)
    local_w2 = lax.dot_general(spread, hidden, row_dims, preferred_element_type=jnp.float32)
    grad_w1, grad_w2 = (
        lax.psum_scatter(local_w1, "tile", scatter_dimension=0, tiled=True),
        lax.psum_scatter(local_w2, "tile", scatter_dimension=0, tiled=True),
    )
    return (grad_w1, grad_w2, loss[None])


def solution(mesh):
    placed = (
        P(("slide", "tile"), None, None),
        P(),
        P(),
        P(),
        P(),
        P(),
        P(),
        P(("slide", "tile")),
        P("slide"),
    )
    return jax.shard_map(
        body,
        mesh=mesh,
        in_specs=placed,
        out_specs=(P(("slide", "tile"), None), P(("slide", "tile"), None), P("slide")),
        check_vma=False,
    )
```

profile of v0, /device:TPU:6, one launch (start us, length us, event | category | flops | bytes accessed | tf_op | source)
XLA Modules:
  0.0 367.7 jit_solution(2572654064017642908)
XLA Ops:
  7.2 0.0 copy-start
  7.2 0.0 all-gather.2.cloned.1.call-start
  7.2 0.0 copy-start.6
  7.2 0.0 copy-start.7
  7.2 2.5 fusion.6
  9.8 0.0 copy-done.6
  9.8 0.0 copy-done.7
  9.8 0.0 copy-start.8
  9.8 0.0 copy-start.5
  9.8 0.0 copy-start.2
  9.8 0.0 copy-start.4
  9.9 1.1 bitcast_reduce_fusion
  10.9 0.0 copy-done.8
  10.9 0.7 multiply_convert_fusion
  11.6 0.0 all-gather.2.cloned.1.call-update
  11.6 0.0 reduce-scatter.7.cloned.1.call-start
  12.3 1.3 dynamic-slice
  14.2 0.0 copy-done.5
  14.3 0.6 reduce_sum.115
  14.9 0.2 dynamic-update-slice
  15.1 104.4 %all-reduce = bf16[2048]{0:T(1024)(128)(2,1)S(1)} all-reduce(bf16[2048]{0:T(1024)(128)(2,1)S(1)} %dynamic-update-slice), channel_id=1, replica_groups=mesh['slide'=16,'tile'=32] {'tile'}, use_global_device_ids=true, to_apply=%add | all-reduce | flops 2048 | bytes 8192
  119.5 0.0 copy-done
  119.5 1.1 fusion.12
  120.6 0.0 copy-done.2
  120.7 0.0 copy-done.4
  120.7 1.2 multiply_reduce_fusion.2
  121.9 0.0 all-gather.2.cloned.1.call-done
  121.9 0.0 copy-start.1
  121.9 3.9 %fusion.4 = f32[2048,256]{0,1:T(8,128)S(1)} fusion(bf16[2048,1024]{1,0:T(8,128)(2,1)} %all-gather.2.cloned.1.call-done, bf16[1024,256]{1,0:T(8,128)(2,1)S(1)} %copy-done), kind=kOutput, calls=%fused_computation.9 | convolution fusion | flops 1075314688 | bytes 6815744 | tf_op jit(solution)/shard_map/dot_general | solution.py:9
  125.9 0.0 copy-done.1
  125.9 1.4 fusion.5
  127.3 0.6 fusion.35
  127.9 0.0 copy-start.3
  127.9 0.9 multiply_reduce_fusion
  128.8 0.7 broadcast_divide_fusion
  129.4 0.0 copy-done.3
  129.5 0.1 multiply_reduce_fusion.4
  129.6 1.3 multiply_reduce_fusion.6
  131.5 0.1 multiply_reduce_fusion.3
  131.6 1.3 multiply_reduce_fusion.5
  132.9 0.1 multiply_reduce_fusion.1
  133.0 1.3 subtract_multiply_fusion
  134.3 0.3 convolution_add_fusion.1
  134.6 0.3 fusion.9
  134.9 0.3 broadcast_in_dim.4
  135.2 5.2 %convolution_bitcast_fusion = f32[1024,256]{0,1:T(8,128)} fusion(bf16[1024,1024]{1,0:T(8,128)(2,1)} %bitcast.34, bf16[1024,1024]{1,0:T(8,128)(2,1)S(1)} %bitcast.31, bf16[1024,256]{1,0:T(8,128)(2,1)} %param.11, bf16[1024,256]{1,0:T(8,128)(2,1)} %copy-done.8), kind=kOutput, calls=%fused_computation.11 | convolution fusion | flops 1074528256 | bytes 6291456 | tf_op jit(solution)/shard_map/dot_general | solution.py:76
  140.4 0.0 copy-start.9
  140.4 2.6 copy.14
  143.0 0.0 reduce-scatter.7.cloned.1.call-update
  143.0 0.0 reduce-scatter.5.cloned.1.call-start
  143.1 0.0 copy-done.9
  143.1 1.8 fusion.36
  144.9 0.0 reduce-scatter.5.cloned.1.call-update
  145.5 101.2 %reduce-scatter.7.cloned.1.call-done = f32[32,256]{1,0:T(8,128)} async-done(((f32[1024,256]{1,0:T(8,128)}), f32[32,256]{1,0:T(8,128)}) %reduce-scatter.7.cloned.1.call-update) | async-done | bytes 32784
  246.8 113.3 %reduce-scatter.5.cloned.1.call-done = f32[32,256]{1,0:T(8,128)} async-done(((f32[1024,256]{1,0:T(8,128)}), f32[32,256]{1,0:T(8,128)}) %reduce-scatter.5.cloned.1.call-update) | async-done | bytes 32784 | tf_op jit(solution)/shard_map/reduce_scatter | solution.py:80
  (3 shorter events, 0.0 us)
Async XLA Ops:
  7.2 112.3 %copy-start = (bf16[1024,256]{1,0:T(8,128)(2,1)S(1)}, bf16[1024,256]{1,0:T(8,128)(2,1)}, u32[]{:S(2)}) copy-start(bf16[1024,256]{1,0:T(8,128)(2,1)} %param.13) | copy-start | bytes 1572868
  7.2 114.7 %all-gather.2.cloned.1.call-start = ((), (), s32[]{:S(2)}) async-start(), calls=%async_computation.2 | async-start | bytes 4325376 | tf_op jit(solution)/shard_map/all_gather | solution.py:41
  7.2 2.6 copy-start.6
  7.2 2.6 copy-start.7
  9.8 1.1 copy-start.8
  9.8 4.4 %copy-start.5 = (f32[2]{0:T(128)S(1)}, f32[2]{0:T(128)}, u32[]{:S(2)}) copy-start(f32[2]{0:T(128)} %param.17) | copy-start | bytes 28
  9.8 110.8 %copy-start.2 = (bf16[1024,256]{1,0:T(8,128)(2,1)S(1)}, bf16[1024,256]{1,0:T(8,128)(2,1)}, u32[]{:S(2)}) copy-start(bf16[1024,256]{1,0:T(8,128)(2,1)} %param.12) | copy-start | bytes 1572868
  9.8 110.8 %copy-start.4 = (f32[256]{0:T(256)S(1)}, f32[256]{0:T(256)}, u32[]{:S(2)}) copy-start(f32[256]{0:T(256)} %param.14) | copy-start | bytes 3076
  11.6 235.1 %reduce-scatter.7.cloned.1.call-start = ((), (), s32[]{:S(2)}) async-start(), calls=%async_computation.4 | async-start | bytes 1081344
  121.9 4.0 %copy-start.1 = (bf16[2048,1024]{1,0:T(8,128)(2,1)S(1)}, bf16[2048,1024]{1,0:T(8,128)(2,1)}, u32[]{:S(2)}) copy-start(bf16[2048,1024]{1,0:T(8,128)(2,1)} %all-gather.2.cloned.1.call-done) | copy-start | bytes 12582916
  127.9 1.5 copy-start.3
  140.4 2.7 copy-start.9
  143.0 217.0 %reduce-scatter.5.cloned.1.call-start = ((), (), s32[]{:S(2)}) async-start(), calls=%async_computation.3 | async-start | bytes 1081344 | tf_op jit(solution)/shard_map/reduce_scatter | solution.py:80
Sparse Core Ops, SparseCore 0:
  11.7 100.6 all-gather.1
  143.1 103.5 reduce-scatter.6
  252.3 107.6 reduce-scatter.4
where the time goes:
time: 368 us
  waiting for transfers between devices  215 us (58%)
  blocking collectives  104 us (28%)
  matrix products  18.8 us (5%)
  between operations  17.7 us (5%)
  other arithmetic  7.6 us (2%)
  local copies, waits for them, and re-layouts  4.43 us (1%)
    reduce_scatter x1, waiting for transfers between devices, body(): lax.psum_scatter(local_w2, 'tile', scatter_dimension=0, tiled=True)  113 us
    unnamed x1, blocking collectives  104 us
    unnamed x4, waiting for transfers between devices  101 us
  transfers between devices with their start and end apart: 3, of which 2 were waited for; matrix products, arithmetic and copies ran while one was open for 2% of the time, Pallas kernels for 0%

commit v1 on v0

v1 whole, which is shorter than its diff:
```python
import functools

import jax
import jax.numpy as jnp
from jax import lax
from jax.experimental import pallas as pl
from jax.experimental.pallas import tpu as pltpu
from jax.sharding import PartitionSpec as P

F32 = jnp.float32
BF16 = jnp.bfloat16
NY, NZ, NC = 4, 4, 2
ROWS = 32
PART = 4 * ROWS
NOTE = 16
VMEM_LIMIT = 48 * 1024 * 1024


def dot(a, b, dims):
    return lax.dot_general(a, b, (dims, ((), ())), preferred_element_type=F32)


def split3(x):
    high = x.astype(BF16)
    rest = x - high.astype(F32)
    mid = rest.astype(BF16)
    low = (rest - mid.astype(F32)).astype(BF16)
    return [high.astype(F32), mid.astype(F32), low.astype(F32)]


def note_rows(total, mean0, mean1):
    rows = split3(total) + split3(mean0) + split3(mean1)
    rows.append(jnp.zeros((NOTE - len(rows), rows[0].shape[1]), F32))
    return jnp.concatenate(rows, axis=0).astype(BF16)


def read_note(note):
    rows = note.astype(F32)
    return [rows[i : i + 1] + rows[i + 1 : i + 2] + rows[i + 2 : i + 3] for i in (0, 3, 6)]


def merge_notes(notes):
    total = sum(n[0] for n in notes)
    shares = [n[0] / total for n in notes]
    mean0 = sum(a * n[1] for a, n in zip(shares, notes))
    mean1 = sum(a * n[2] for a, n in zip(shares, notes))
    offsets = [(n[1] - n[2]) - (mean0 - mean1) for n in notes]
    return total, mean0, mean1, shares, offsets


def local_kernel(
    count_ref,
    tiles_ref,
    w_reduce_ref,
    w_expand_ref,
    att_tanh_ref,
    att_gate_ref,
    att_vector_ref,
    classifier_ref,
    keep_ref,
    send_ref,
):
    rows, width = tiles_ref.shape
    slots = rows // 16
    flat = tiles_ref[...]
    hidden = jnp.maximum(dot(flat, w_reduce_ref[...], ((1,), (0,))), 0.0).astype(BF16)
    tile_of = lax.broadcasted_iota(jnp.int32, (slots, rows), 0)
    row_of = lax.broadcasted_iota(jnp.int32, (slots, rows), 1)
    pool = (tile_of == lax.shift_right_logical(row_of, 4)).astype(F32).astype(BF16)
    tile_sum = dot(pool, flat, ((1,), (0,)))
    hidden_sum = dot(pool, hidden, ((1,), (0,)))
    sum_high = hidden_sum.astype(BF16)
    sum_low = (hidden_sum - sum_high.astype(F32)).astype(BF16)
    w_expand = w_expand_ref[...]
    expanded = dot(jnp.concatenate([sum_high, sum_low], axis=0), w_expand, ((1,), (1,)))
    embed = ((tile_sum + expanded[:slots] + expanded[slots:]) * (1.0 / 16.0)).astype(BF16)
    att_tanh, att_gate = att_tanh_ref[...], att_gate_ref[...]
    tanh_part = jnp.tanh(dot(embed, att_tanh, ((1,), (0,))))
    gate_part = jax.nn.sigmoid(dot(embed, att_gate, ((1,), (0,))))
    vector = att_vector_ref[...]
    score = jnp.sum(tanh_part * gate_part * vector, axis=1, keepdims=True)
    slot = lax.broadcasted_iota(jnp.int32, (slots, 1), 0)
    weight = jnp.where(slot < count_ref[0], jnp.exp(score), 0.0)
    total = jnp.sum(weight, axis=0, keepdims=True)
    share = weight / total
    embed_float = embed.astype(F32)
    class0, class1 = classifier_ref[0:1, :], classifier_ref[1:2, :]
    u0 = jnp.sum(embed_float * class0, axis=1, keepdims=True)
    u1 = jnp.sum(embed_float * class1, axis=1, keepdims=True)
    mean0 = jnp.sum(share * u0, axis=0, keepdims=True)
    mean1 = jnp.sum(share * u1, axis=0, keepdims=True)
    slope = share * ((u0 - u1) - (mean0 - mean1))
    e_tanh = (vector * gate_part * (1.0 - tanh_part * tanh_part)).astype(BF16)
    e_gate = (vector * tanh_part * gate_part * (1.0 - gate_part)).astype(BF16)
    path = dot(e_tanh, att_tanh, ((1,), (1,))) + dot(e_gate, att_gate, ((1,), (1,)))
    dy_a = ((share * (class0 - class1) + slope * path) * (1.0 / 16.0)).astype(BF16)
    dy_b = (share * path * (1.0 / 16.0)).astype(BF16)
    dy = jnp.concatenate([dy_a, dy_b], axis=0)
    back = dot(dy, w_expand, ((1,), (0,))).astype(BF16)
    back = jnp.concatenate([back[:slots], back[slots:]], axis=1)
    spread = dot(pool, back, ((0,), (0,)))
    hid = hidden.shape[1]
    mask = hidden.astype(F32) > 0
    dhid = jnp.concatenate(
        [jnp.where(mask, spread[:, :hid], 0.0), jnp.where(mask, spread[:, hid:], 0.0)], axis=1
    ).astype(BF16)
    grad_w1 = dot(flat, dhid, ((0,), (0,)))
    sums = jnp.concatenate([sum_high, sum_low], axis=0)
    w2_a = dot(jnp.concatenate([dy_a, dy_a], axis=0), sums, ((0,), (0,)))
    w2_b = dot(jnp.concatenate([dy_b, dy_b], axis=0), sums, ((0,), (0,)))
    first = lax.rem(lax.axis_index("tile"), NC) == 0
    parts = [grad_w1[:, :hid], w2_a, grad_w1[:, hid:], w2_b]
    note = note_rows(*[jnp.broadcast_to(v, (1, hid)) for v in (total, mean0, mean1)])
    for y in range(NY):
        for z in range(NZ):
            for i, part in enumerate(parts):
                at = (y * NZ + z) * NC * ROWS
                even = part[at : at + ROWS].astype(BF16)
                odd = part[at + ROWS : at + 2 * ROWS].astype(BF16)
                here = pl.ds(z * PART + i * ROWS, ROWS)
                keep_ref[y, here, :] = jnp.where(first, even, odd)
                send_ref[y, here, :] = jnp.where(first, odd, even)
        keep_ref[y, NZ * PART :, :] = note
        send_ref[y, NZ * PART :, :] = note


def merge(blocks, notes):
    total, mean0, mean1, shares, offsets = merge_notes(notes)
    sums = []
    for i in (0, 1):
        sums.append(sum(a * (b[i] + o * b[i + 2]) for a, o, b in zip(shares, offsets, blocks)))
    for i in (2, 3):
        sums.append(sum(a * b[i] for a, b in zip(shares, blocks)))
    return sums, note_rows(total, mean0, mean1)


def core_kernel(own_ref, other_ref, out_ref):
    tail = NZ * PART
    notes = [read_note(r[0, tail:, :]) for r in (own_ref, other_ref)]
    for y in range(NY):
        for z in range(NZ):
            blocks = [
                [r[y, z * PART + i * ROWS : z * PART + (i + 1) * ROWS, :].astype(F32) for i in range(4)]
                for r in (own_ref, other_ref)
            ]
            sums, note = merge(blocks, notes)
            for i in range(4):
                out_ref[y, pl.ds(z * PART + i * ROWS, ROWS), :] = sums[i].astype(BF16)
        out_ref[y, tail:, :] = note


def y_kernel(in_ref, out_ref):
    tail = NZ * PART
    notes = [read_note(in_ref[y, tail:, :]) for y in range(NY)]
    for z in range(NZ):
        blocks = [
            [in_ref[y, z * PART + i * ROWS : z * PART + (i + 1) * ROWS, :].astype(F32) for i in range(4)]
            for y in range(NY)
        ]
        sums, note = merge(blocks, notes)
        for i in range(4):
            out_ref[z, pl.ds(i * ROWS, ROWS), :] = sums[i].astype(BF16)
        out_ref[z, PART:, :] = note


def z_kernel(count, in_ref, target_ref, w1_ref, w2_ref, loss_ref):
    notes = [read_note(in_ref[z, PART:, :]) for z in range(NZ)]
    total, mean0, mean1, shares, offsets = merge_notes(notes)
    width = mean0.shape[1]
    target0 = jnp.full((1, width), target_ref[0], F32)
    target1 = jnp.full((1, width), target_ref[1], F32)
    target_sum = target0 + target1
    share0, share1 = target0 / target_sum, target1 / target_sum
    log_partition_sum = jnp.log(jnp.exp(mean0) + jnp.exp(mean1))
    loss = log_partition_sum - (mean0 * share0 + mean1 * share1)
    scale = count * (jnp.exp(mean0 - log_partition_sum) - share0)
    loss_ref[...] = loss[:, :128]
    for i, out_ref in enumerate((w1_ref, w2_ref)):
        result = 0.0
        for z in range(NZ):
            a = in_ref[z, i * ROWS : (i + 1) * ROWS, :].astype(F32)
            b = in_ref[z, (i + 2) * ROWS : (i + 3) * ROWS, :].astype(F32)
            result = result + shares[z] * (a + offsets[z] * b)
        out_ref[...] = scale * result


def vmem(count):
    return [pl.BlockSpec(memory_space=pltpu.VMEM)] * count


def call(kernel, out_shape, in_specs, args, name):
    many = isinstance(out_shape, (tuple, list))
    return pl.pallas_call(
        kernel,
        out_shape=out_shape,
        in_specs=in_specs,
        out_specs=tuple(vmem(len(out_shape))) if many else vmem(1)[0],
        compiler_params=pltpu.CompilerParams(vmem_limit_bytes=VMEM_LIMIT),
        name=name,
    )(*args)


def place(y, z, core):
    return (y * NZ + z) * NC + core


def body(
    tiles,
    w_reduce,
    w_expand,
    att_tanh,
    att_gate,
    att_vector,
    classifier,
    tile_counts,
    target_weights,
):
    slots, positions, width = tiles.shape
    hid = w_reduce.shape[1]
    smem = pl.BlockSpec(memory_space=pltpu.SMEM)
    chunk = jax.ShapeDtypeStruct((NY, NZ * PART + NOTE, hid), BF16)
    keep, send = call(
        local_kernel,
        (chunk, chunk),
        [smem] + vmem(7),
        (
            tile_counts,
            tiles.reshape(slots * positions, width),
            w_reduce,
            w_expand,
            att_tanh,
            att_gate,
            att_vector.reshape(1, hid),
            classifier.T,
        ),
        "local",
    )
    everyone = [(y, z, c) for y in range(NY) for z in range(NZ) for c in range(NC)]
    other = lax.ppermute(send, "tile", [(place(y, z, c), place(y, z, 1 - c)) for y, z, c in everyone])
    pair = call(core_kernel, chunk, vmem(2), (keep, other), "join_cores")
    along_y = [[place(y, z, c) for y in range(NY)] for z in range(NZ) for c in range(NC)]
    along_z = [[place(y, z, c) for z in range(NZ)] for y in range(NY) for c in range(NC)]
    pair = lax.all_to_all(pair, "tile", 0, 0, axis_index_groups=along_y, tiled=True)
    line = call(
        y_kernel, jax.ShapeDtypeStruct((NZ, PART + NOTE, hid), BF16), vmem(1), (pair,), "join_y"
    )
    line = lax.all_to_all(line, "tile", 0, 0, axis_index_groups=along_z, tiled=True)
    count = float(lax.axis_size("tile") * slots // 2)
    out = jax.ShapeDtypeStruct((ROWS, hid), F32)
    grad_w1, grad_w2, loss = call(
        functools.partial(z_kernel, count),
        (out, out, jax.ShapeDtypeStruct((1, 128), F32)),
        vmem(1) + [smem],
        (line, target_weights),
        "join_z",
    )
    return grad_w1, grad_w2, loss[0, :1]


def solution(mesh):
    placed = (
        P(("slide", "tile"), None, None),
        P(),
        P(),
        P(),
        P(),
        P(),
        P(),
        P(("slide", "tile")),
        P("slide"),
    )
    return jax.shard_map(
        body,
        mesh=mesh,
        in_specs=placed,
        out_specs=(P(("slide", "tile"), None), P(("slide", "tile"), None), P("slide")),
        check_vma=False,
    )
```

time: 368 us -> 76.8 us (0.21)
  the two profiles are of different devices: /device:TPU:6 before, /device:TPU:36 now
where the time goes in v1:
time: 76.8 us; the launch traced here: 76.3 us
  blocking collectives  56.3 us (73%)
  Pallas kernels  8.61 us (11%)
  local copies, waits for them, and re-layouts  5.54 us (7%)
  waiting for transfers between devices  2.67 us (3%)
  starting transfers between devices  1.92 us (2%)
  between operations  1.32 us (2%)
    all_to_all x1, blocking collectives, body(): lax.all_to_all(line, 'tile', 0, 0, axis_index_groups=along_z, tiled=True)  36.3 us
    all_to_all x1, blocking collectives, body(): lax.all_to_all(pair, 'tile', 0, 0, axis_index_groups=along_y, tiled=True)  20 us
    pallas_call x4, Pallas kernels, call(): pl.pallas_call(kernel, out_shape=out_shape, in_specs=in_specs, out_specs=...  8.61 us
    unnamed x14, local copies, waits for them, and re-layouts  5.54 us
    ppermute x1, waiting for transfers between devices, body(): lax.ppermute(send, 'tile', [(place(y, z, c), place(y, z, 1 - c)) for y, z...  2.67 us
    ppermute x1, starting transfers between devices, body(): lax.ppermute(send, 'tile', [(place(y, z, c), place(y, z, 1 - c)) for y, z...  1.92 us
  transfers between devices with their start and end apart: 1, of which 1 were waited for; matrix products, arithmetic and copies ran while one was open for 0% of the time, Pallas kernels for 0%

profile of v1, /device:TPU:36, one launch (start us, length us, event | category | flops | bytes accessed | tf_op | source)
XLA Modules:
  0.0 76.3 jit_solution(14872831779632052098)
XLA Ops:
  1.3 0.0 copy-start
  1.3 1.0 %copy-done = bf16[1024,256]{1,0:T(8,128)(2,1)S(1)} copy-done((bf16[1024,256]{1,0:T(8,128)(2,1)S(1)}, bf16[1024,256]{1,0:T(8,128)(2,1)}, u32[]{:S(2)}) %copy-start) | copy-done | bytes 524312
  2.3 0.0 copy-start.1
  2.3 1.0 %copy-done.1 = bf16[1024,256]{1,0:T(8,128)(2,1)S(1)} copy-done((bf16[1024,256]{1,0:T(8,128)(2,1)S(1)}, bf16[1024,256]{1,0:T(8,128)(2,1)}, u32[]{:S(2)}) %copy-start.1) | copy-done | bytes 524312
  3.4 0.0 copy-start.2
  3.4 1.0 %copy-done.2 = bf16[1024,256]{1,0:T(8,128)(2,1)S(1)} copy-done((bf16[1024,256]{1,0:T(8,128)(2,1)S(1)}, bf16[1024,256]{1,0:T(8,128)(2,1)}, u32[]{:S(2)}) %copy-start.2) | copy-done | bytes 524312
  4.4 0.0 copy-start.3
  4.4 1.0 %copy-done.3 = bf16[1024,256]{1,0:T(8,128)(2,1)S(1)} copy-done((bf16[1024,256]{1,0:T(8,128)(2,1)S(1)}, bf16[1024,256]{1,0:T(8,128)(2,1)}, u32[]{:S(2)}) %copy-start.3) | copy-done | bytes 524312
  5.4 0.0 copy-start.4
  5.5 0.7 copy-done.4
  6.1 0.0 copy-start.5
  6.1 0.7 copy-done.5
  6.8 6.4 %local.1 = (bf16[4,528,256]{2,1,0:T(8,128)(2,1)S(1)}, bf16[4,528,256]{2,1,0:T(8,128)(2,1)S(1)}) custom-call(s32[1]{0:T(128)S(6)} %copy.12.count_ref, bf16[1024,1024]{1,0:T(8,128)(2,1)} %bitcast.7, bf16[1024,256]{1,0:T(8,128)(2,1)S(1)} %copy-done, bf16[1024,256]{1,0:T(8,128)(2,1)S(1)} %copy-done.1, bf16[1024,256]{1,0:T(8,128)(2,1)S(1)} %copy-done.2, ...), custom_call_target="tpu_custom_call" | custom-call | tf_op jit(solution)/shard_map/local/pallas_call | solution.py:193
  13.3 1.9 %collective-permute-start = (bf16[4,528,256]{2,1,0:T(8,128)(2,1)S(1)}, bf16[4,528,256]{2,1,0:T(8,128)(2,1)S(1)}, u32[]{:S(2)}, u32[]{:S(2)}) collective-permute-start(bf16[4,528,256]{2,1,0:T(8,128)(2,1)S(1)} %get-tuple-element.9), channel_id=1, source_target_pairs={{0,1},{1,0},{2,3},{3,2},{4,5},{5,4},{6,7},{7,6},{8,9},{9,8},{10,11... | collective-permute-start | bytes 3244040 | tf_op jit(solution)/shard_map/ppermute | solution.py:239
  15.2 2.7 %collective-permute-done.other_ref = bf16[4,528,256]{2,1,0:T(8,128)(2,1)S(1)} collective-permute-done((bf16[4,528,256]{2,1,0:T(8,128)(2,1)S(1)}, bf16[4,528,256]{2,1,0:T(8,128)(2,1)S(1)}, u32[]{:S(2)}, u32[]{:S(2)}) %collective-permute-start) | collective-permute-done | bytes 1081376 | tf_op jit(solution)/shard_map/ppermute | solution.py:239
  17.9 0.6 join_cores.1
  18.5 20.0 %all_to_all.10.in_ref = bf16[4,528,256]{2,1,0:T(8,128)(2,1)S(1)} all-to-all(bf16[4,528,256]{2,1,0:T(8,128)(2,1)S(1)} %join_cores.1), channel_id=1, replica_groups={{0,8,16,24},{1,9,17,25},{2,10,18,26},{3,11,19,27},{4,12,20,28},{5,13,21..., dimensions={0} | all-to-all | bytes 2162688 | tf_op jit(solution)/shard_map/all_to_all | solution.py:243
  38.5 0.0 copy-start.6
  38.5 0.3 join_y.1
  38.8 36.3 %all_to_all.11.in_ref = bf16[4,144,256]{2,1,0:T(8,128)(2,1)S(1)} all-to-all(bf16[4,144,256]{2,1,0:T(8,128)(2,1)S(1)} %join_y.1), channel_id=1, replica_groups={{0,2,4,6},{1,3,5,7},{8,10,12,14},{9,11,13,15},{16,18,20,22},{17,19,21,2..., dimensions={0} | all-to-all | bytes 589824 | tf_op jit(solution)/shard_map/all_to_all | solution.py:247
  75.1 0.0 copy-done.6
  75.1 1.2 %join_z.1 = (f32[32,256]{1,0:T(8,128)}, f32[32,256]{1,0:T(8,128)}, f32[1,128]{1,0:T(1,128)}) custom-call(bf16[4,144,256]{2,1,0:T(8,128)(2,1)S(1)} %all_to_all.11.in_ref, f32[2]{0:T(128)S(1)} %copy-done.6), custom_call_target="tpu_custom_call" | custom-call | tf_op jit(solution)/shard_map/join_z/pallas_call | solution.py:193
Async XLA Ops:
  1.3 1.0 %copy-start = (bf16[1024,256]{1,0:T(8,128)(2,1)S(1)}, bf16[1024,256]{1,0:T(8,128)(2,1)}, u32[]{:S(2)}) copy-start(bf16[1024,256]{1,0:T(8,128)(2,1)} %w_reduce_ref.1) | copy-start | bytes 1572868
  2.3 1.0 %copy-start.1 = (bf16[1024,256]{1,0:T(8,128)(2,1)S(1)}, bf16[1024,256]{1,0:T(8,128)(2,1)}, u32[]{:S(2)}) copy-start(bf16[1024,256]{1,0:T(8,128)(2,1)} %w_expand_ref.1) | copy-start | bytes 1572868
  3.4 1.0 %copy-start.2 = (bf16[1024,256]{1,0:T(8,128)(2,1)S(1)}, bf16[1024,256]{1,0:T(8,128)(2,1)}, u32[]{:S(2)}) copy-start(bf16[1024,256]{1,0:T(8,128)(2,1)} %att_tanh_ref.1) | copy-start | bytes 1572868
  4.4 1.0 %copy-start.3 = (bf16[1024,256]{1,0:T(8,128)(2,1)S(1)}, bf16[1024,256]{1,0:T(8,128)(2,1)}, u32[]{:S(2)}) copy-start(bf16[1024,256]{1,0:T(8,128)(2,1)} %att_gate_ref.1) | copy-start | bytes 1572868
  5.4 0.7 copy-start.4
  6.1 0.7 copy-start.5
  13.3 4.6 %collective-permute-start = (bf16[4,528,256]{2,1,0:T(8,128)(2,1)S(1)}, bf16[4,528,256]{2,1,0:T(8,128)(2,1)S(1)}, u32[]{:S(2)}, u32[]{:S(2)}) collective-permute-start(bf16[4,528,256]{2,1,0:T(8,128)(2,1)S(1)} %get-tuple-element.9), channel_id=1, source_target_pairs={{0,1},{1,0},{2,3},{3,2},{4,5},{5,4},{6,7},{7,6},{8,9},{9,8},{10,11... | collective-permute-start | bytes 3244040 | tf_op jit(solution)/shard_map/ppermute | solution.py:239
  38.5 36.6 %copy-start.6 = (f32[2]{0:T(128)S(1)}, f32[2]{0:T(128)}, u32[]{:S(2)}) copy-start(f32[2]{0:T(128)} %target_ref.1) | copy-start | bytes 28

commit v2 on v1

v2 whole, which is shorter than its diff:
```python
import functools

import jax
import jax.numpy as jnp
from jax import lax
from jax.experimental import pallas as pl
from jax.experimental.pallas import tpu as pltpu
from jax.sharding import PartitionSpec as P

F32 = jnp.float32
BF16 = jnp.bfloat16
NY, NZ, NC = 4, 4, 2
ROWS = 32
PART = 8 * ROWS
HALF = PART // 2
TAIL = NZ * PART
NOTE = 16
VMEM_LIMIT = 48 * 1024 * 1024


def dot(a, b, dims):
    return lax.dot_general(a, b, (dims, ((), ())), preferred_element_type=F32)


def split3(x):
    high = x.astype(BF16)
    rest = x - high.astype(F32)
    mid = rest.astype(BF16)
    low = (rest - mid.astype(F32)).astype(BF16)
    return [high.astype(F32), mid.astype(F32), low.astype(F32)]


def note_rows(total, mean0, mean1):
    rows = split3(total) + split3(mean0) + split3(mean1)
    rows.append(jnp.zeros((NOTE - len(rows), rows[0].shape[1]), F32))
    return jnp.concatenate(rows, axis=0).astype(BF16)


def read_note(note):
    rows = note.astype(F32)
    return [rows[i : i + 1] + rows[i + 1 : i + 2] + rows[i + 2 : i + 3] for i in (0, 3, 6)]


def merge_notes(notes):
    total = sum(n[0] for n in notes)
    shares = [n[0] / total for n in notes]
    mean0 = sum(a * n[1] for a, n in zip(shares, notes))
    mean1 = sum(a * n[2] for a, n in zip(shares, notes))
    offsets = [(n[1] - n[2]) - (mean0 - mean1) for n in notes]
    return total, mean0, mean1, shares, offsets


def position_sum(x):
    return jnp.sum(x.reshape(x.shape[0] // 16, 16, x.shape[1]).astype(F32), axis=1)


def store_parts(part_a, part_b, which, keep_ref, send_ref):
    first = lax.rem(lax.axis_index("tile"), NC) == 0
    for y in range(NY):
        for z in range(NZ):
            at = (y * NZ + z) * NC * ROWS
            for i, part in enumerate((part_a, part_b)):
                for half in range(2):
                    cols = slice(half * 128, half * 128 + 128)
                    even = part[at : at + ROWS, cols].astype(BF16)
                    odd = part[at + ROWS : at + 2 * ROWS, cols].astype(BF16)
                    here = pl.ds(z * PART + (4 * i + 2 * which + half) * ROWS, ROWS)
                    keep_ref[y, here, :] = jnp.where(first, even, odd)
                    send_ref[y, here, :] = jnp.where(first, odd, even)


CHUNKS = 2


def local_kernel(
    count_ref,
    tiles_hbm,
    w_reduce_hbm,
    w_expand_hbm,
    att_tanh_hbm,
    att_gate_hbm,
    att_vector_hbm,
    classifier_hbm,
    keep_ref,
    send_ref,
    flat_ref,
    w_reduce_ref,
    w_expand_ref,
    att_tanh_ref,
    att_gate_ref,
    att_vector_ref,
    classifier_ref,
    hidden_ref,
    sem,
):
    rows, width = flat_ref.shape
    slots = rows // 16
    step = rows // CHUNKS
    copies = [pltpu.make_async_copy(w_reduce_hbm, w_reduce_ref, sem.at[CHUNKS])]
    for i in range(CHUNKS):
        part = pl.ds(i * step, step)
        copies.append(pltpu.make_async_copy(tiles_hbm.at[part], flat_ref.at[part], sem.at[i]))
    copies.append(pltpu.make_async_copy(w_expand_hbm, w_expand_ref, sem.at[CHUNKS + 1]))
    copies.append(pltpu.make_async_copy(att_tanh_hbm, att_tanh_ref, sem.at[CHUNKS + 2]))
    copies.append(pltpu.make_async_copy(att_gate_hbm, att_gate_ref, sem.at[CHUNKS + 3]))
    copies.append(pltpu.make_async_copy(att_vector_hbm, att_vector_ref, sem.at[CHUNKS + 4]))
    copies.append(pltpu.make_async_copy(classifier_hbm, classifier_ref, sem.at[CHUNKS + 5]))
    for copy in copies:
        copy.start()
    copies[0].wait()
    w_reduce = w_reduce_ref[...]
    tile_sums, hidden_sums = [], []
    for i in range(CHUNKS):
        copies[1 + i].wait()
        part = pl.ds(i * step, step)
        flat = flat_ref[part, :]
        hidden = jnp.maximum(dot(flat, w_reduce, ((1,), (0,))), 0.0).astype(BF16)
        hidden_ref[part, :] = hidden
        tile_sums.append(position_sum(flat))
        hidden_sums.append(position_sum(hidden))
    tile_sum = jnp.concatenate(tile_sums, axis=0)
    hidden_sum = jnp.concatenate(hidden_sums, axis=0)
    sum_high = hidden_sum.astype(BF16)
    sum_low = (hidden_sum - sum_high.astype(F32)).astype(BF16)
    copies[CHUNKS + 1].wait()
    w_expand = w_expand_ref[...]
    sums = jnp.concatenate([sum_high, sum_low], axis=0)
    expanded = dot(sums, w_expand, ((1,), (1,)))
    embed = ((tile_sum + expanded[:slots] + expanded[slots:]) * (1.0 / 16.0)).astype(BF16)
    for copy in copies[CHUNKS + 2 :]:
        copy.wait()
    att_tanh, att_gate = att_tanh_ref[...], att_gate_ref[...]
    tanh_part = jnp.tanh(dot(embed, att_tanh, ((1,), (0,))))
    gate_part = jax.nn.sigmoid(dot(embed, att_gate, ((1,), (0,))))
    vector = att_vector_ref[...]
    score = jnp.sum(tanh_part * gate_part * vector, axis=1, keepdims=True)
    slot = lax.broadcasted_iota(jnp.int32, (slots, 1), 0)
    weight = jnp.where(slot < count_ref[0], jnp.exp(score), 0.0)
    total = jnp.sum(weight, axis=0, keepdims=True)
    share = weight / total
    embed_float = embed.astype(F32)
    class0, class1 = classifier_ref[0:1, :], classifier_ref[1:2, :]
    u0 = jnp.sum(embed_float * class0, axis=1, keepdims=True)
    u1 = jnp.sum(embed_float * class1, axis=1, keepdims=True)
    mean0 = jnp.sum(share * u0, axis=0, keepdims=True)
    mean1 = jnp.sum(share * u1, axis=0, keepdims=True)
    slope = share * ((u0 - u1) - (mean0 - mean1))
    e_tanh = (vector * gate_part * (1.0 - tanh_part * tanh_part)).astype(BF16)
    e_gate = (vector * tanh_part * gate_part * (1.0 - gate_part)).astype(BF16)
    path = dot(e_tanh, att_tanh, ((1,), (1,))) + dot(e_gate, att_gate, ((1,), (1,)))
    dy_a = ((share * (class0 - class1) + slope * path) * (1.0 / 16.0)).astype(BF16)
    dy_b = (share * path * (1.0 / 16.0)).astype(BF16)
    w2_a = dot(jnp.concatenate([dy_a, dy_a], axis=0), sums, ((0,), (0,)))
    w2_b = dot(jnp.concatenate([dy_b, dy_b], axis=0), sums, ((0,), (0,)))
    store_parts(w2_a, w2_b, 1, keep_ref, send_ref)
    note = note_rows(*[jnp.broadcast_to(v, (1, 128)) for v in (total, mean0, mean1)])
    for y in range(NY):
        keep_ref[y, TAIL:, :] = note
        send_ref[y, TAIL:, :] = note
    back = dot(jnp.concatenate([dy_a, dy_b], axis=0), w_expand, ((1,), (0,))).astype(BF16)
    back = jnp.concatenate([back[:slots], back[slots:]], axis=1)
    spread = jnp.broadcast_to(back.astype(F32)[:, None, :], (slots, 16, back.shape[1]))
    spread = spread.reshape(rows, back.shape[1])
    mask = hidden_ref[...].astype(F32) > 0
    hid = mask.shape[1]
    dhid = jnp.concatenate(
        [jnp.where(mask, spread[:, :hid], 0.0), jnp.where(mask, spread[:, hid:], 0.0)], axis=1
    ).astype(BF16)
    grad_w1 = dot(flat_ref[...], dhid, ((0,), (0,)))
    store_parts(grad_w1[:, :hid], grad_w1[:, hid:], 0, keep_ref, send_ref)


def merge(blocks, shares, offsets):
    a = b = 0.0
    for share, offset, block in zip(shares, offsets, blocks):
        block_b = block[HALF:].astype(F32)
        a = a + share * (block[:HALF].astype(F32) + offset * block_b)
        b = b + share * block_b
    return a.astype(BF16), b.astype(BF16)


def core_kernel(own_ref, other_ref, *out_refs):
    notes = [read_note(r[0, TAIL:, :]) for r in (own_ref, other_ref)]
    total, mean0, mean1, shares, offsets = merge_notes(notes)
    note = note_rows(total, mean0, mean1)
    here = lax.div(lax.axis_index("tile"), NZ * NC)
    for away, out_ref in enumerate(out_refs):
        y = lax.rem(here + away, NY)
        for z in range(NZ):
            part = slice(z * PART, (z + 1) * PART)
            a, b = merge([r[y, part, :] for r in (own_ref, other_ref)], shares, offsets)
            out_ref[z * PART : z * PART + HALF, :] = a
            out_ref[z * PART + HALF : (z + 1) * PART, :] = b
        out_ref[TAIL:, :] = note


def y_kernel(in0, in1, in2, in3, *out_refs):
    in_refs = (in0, in1, in2, in3)
    notes = [read_note(r[TAIL:, :]) for r in in_refs]
    total, mean0, mean1, shares, offsets = merge_notes(notes)
    note = note_rows(total, mean0, mean1)
    here = lax.rem(lax.div(lax.axis_index("tile"), NC), NZ)
    for away, out_ref in enumerate(out_refs):
        z = lax.rem(here + away, NZ)
        part = pl.ds(pl.multiple_of(z * PART, PART), PART)
        a, b = merge([r[part, :] for r in in_refs], shares, offsets)
        out_ref[:HALF, :] = a
        out_ref[HALF:PART, :] = b
        out_ref[PART:, :] = note


def z_kernel(count, in0, in1, in2, in3, target_ref, w1_ref, w2_ref, loss_ref):
    in_refs = (in0, in1, in2, in3)
    notes = [read_note(r[PART:, :]) for r in in_refs]
    total, mean0, mean1, shares, offsets = merge_notes(notes)
    width = mean0.shape[1]
    target0 = jnp.full((1, width), target_ref[0], F32)
    target1 = jnp.full((1, width), target_ref[1], F32)
    target_sum = target0 + target1
    share0, share1 = target0 / target_sum, target1 / target_sum
    log_partition_sum = jnp.log(jnp.exp(mean0) + jnp.exp(mean1))
    loss_ref[...] = log_partition_sum - (mean0 * share0 + mean1 * share1)
    scale = count * (jnp.exp(mean0 - log_partition_sum) - share0)
    for i, out_ref in enumerate((w1_ref, w2_ref)):
        result = 0.0
        for share, offset, r in zip(shares, offsets, in_refs):
            a = r[2 * i * ROWS : 2 * (i + 1) * ROWS, :].astype(F32)
            b = r[HALF + 2 * i * ROWS : HALF + 2 * (i + 1) * ROWS, :].astype(F32)
            result = result + share * (a + offset * b)
        result = scale * result
        out_ref[:, :width] = result[:ROWS]
        out_ref[:, width:] = result[ROWS:]


def vmem(count):
    return [pl.BlockSpec(memory_space=pltpu.VMEM)] * count


def call(kernel, out_shape, in_specs, args, name, scratch=()):
    many = isinstance(out_shape, (tuple, list))
    return pl.pallas_call(
        kernel,
        out_shape=out_shape,
        in_specs=in_specs,
        out_specs=tuple(vmem(len(out_shape))) if many else vmem(1)[0],
        scratch_shapes=list(scratch),
        compiler_params=pltpu.CompilerParams(vmem_limit_bytes=VMEM_LIMIT),
        name=name,
    )(*args)


def place(y, z, core):
    return (y * NZ + z) * NC + core


def body(
    tiles,
    w_reduce,
    w_expand,
    att_tanh,
    att_gate,
    att_vector,
    classifier,
    tile_counts,
    target_weights,
):
    slots, positions, width = tiles.shape
    rows = slots * positions
    hid = w_reduce.shape[1]
    smem = pl.BlockSpec(memory_space=pltpu.SMEM)
    hbm = pl.BlockSpec(memory_space=pltpu.HBM)
    held = [
        pltpu.with_memory_space_constraint(x, pltpu.HBM)
        for x in (
            tiles.reshape(rows, width),
            w_reduce,
            w_expand,
            att_tanh,
            att_gate,
            att_vector.reshape(1, hid),
            classifier.T,
        )
    ]
    chunk = jax.ShapeDtypeStruct((NY, TAIL + NOTE, 128), BF16)
    keep, send = call(
        local_kernel,
        (chunk, chunk),
        [smem] + [hbm] * 7,
        (tile_counts, *held),
        "local",
        [pltpu.VMEM((rows, width), BF16)]
        + [pltpu.VMEM((width, hid), BF16)] * 4
        + [pltpu.VMEM((1, hid), F32), pltpu.VMEM((2, width), F32)]
        + [pltpu.VMEM((rows, hid), BF16), pltpu.SemaphoreType.DMA((CHUNKS + 6,))],
    )
    everyone = [(y, z, c) for y in range(NY) for z in range(NZ) for c in range(NC)]

    def move(x, dy, dz, dc):
        pairs = [
            (place(y, z, c), place((y + dy) % NY, (z + dz) % NZ, (c + dc) % NC)) for y, z, c in everyone
        ]
        return lax.ppermute(x, "tile", pairs)

    other = move(send, 0, 0, 1)
    piece = jax.ShapeDtypeStruct((TAIL + NOTE, 128), BF16)
    pieces = call(core_kernel, (piece,) * NY, vmem(2), (keep, other), "join_cores")
    across = [move(pieces[2], 2, 0, 0), move(pieces[1], 1, 0, 0), move(pieces[3], 3, 0, 0)]
    piece = jax.ShapeDtypeStruct((PART + NOTE, 128), BF16)
    pieces = call(y_kernel, (piece,) * NZ, vmem(NY), (pieces[0], *across), "join_y")
    across = [move(pieces[2], 0, 2, 0), move(pieces[1], 0, 1, 0), move(pieces[3], 0, 3, 0)]
    count = float(lax.axis_size("tile") * slots // 2)
    out = jax.ShapeDtypeStruct((ROWS, hid), F32)
    grad_w1, grad_w2, loss = call(
        functools.partial(z_kernel, count),
        (out, out, jax.ShapeDtypeStruct((1, 128), F32)),
        vmem(NZ) + [smem],
        (pieces[0], *across, target_weights),
        "join_z",
    )
    return grad_w1, grad_w2, loss[0, :1]


def solution(mesh):
    placed = (
        P(("slide", "tile"), None, None),
        P(),
        P(),
        P(),
        P(),
        P(),
        P(),
        P(("slide", "tile")),
        P("slide"),
    )
    return jax.shard_map(
        body,
        mesh=mesh,
        in_specs=placed,
        out_specs=(P(("slide", "tile"), None), P(("slide", "tile"), None), P("slide")),
        check_vma=False,
    )
```

time: 76.8 us -> 65 us (0.85)
  the two profiles are of different devices: /device:TPU:36 before, /device:TPU:6 now
where the time goes in v2:
time: 65 us; the launch traced here: 64.8 us
  starting transfers between devices  39.6 us (61%)
  waiting for transfers between devices  16.1 us (25%)
  Pallas kernels  7.75 us (12%)
  between operations  1.37 us (2%)
    ppermute x7, starting transfers between devices, move(): return lax.ppermute(x, 'tile', pairs)  39.6 us
    ppermute x7, waiting for transfers between devices, move(): return lax.ppermute(x, 'tile', pairs)  16.1 us
    pallas_call x4, Pallas kernels, call(): pl.pallas_call(kernel, out_shape=out_shape, in_specs=in_specs, out_specs=...  7.75 us
  transfers between devices with their start and end apart: 7, of which 6 were waited for; matrix products, arithmetic and copies ran while one was open for 0% of the time, Pallas kernels for 0%

profile of v2, /device:TPU:6, one launch (start us, length us, event | category | flops | bytes accessed | tf_op | source)
XLA Modules:
  0.0 64.8 jit_solution(4842290733667078957)
XLA Ops:
  1.3 5.6 %local.1 = (bf16[4,1040,128]{2,1,0:T(8,128)(2,1)S(1)}, bf16[4,1040,128]{2,1,0:T(8,128)(2,1)S(1)}) custom-call(s32[1]{0:T(128)S(6)} %copy.12.count_ref, bf16[1024,1024]{1,0:T(8,128)(2,1)} %bitcast.5, bf16[1024,256]{1,0:T(8,128)(2,1)} %w_reduce_hbm.1, bf16[1024,256]{1,0:T(8,128)(2,1)} %w_expand_hbm.1, bf16[1024,256]{1,0:T(8,128)(2,1)} %att_tanh_hbm.1, ...), custom_call_target="tpu_custom_call" | custom-call | tf_op jit(solution)/shard_map/local/pallas_call | solution.py:241
  6.9 1.9 %collective-permute-start = (bf16[4,1040,128]{2,1,0:T(8,128)(2,1)S(1)}, bf16[4,1040,128]{2,1,0:T(8,128)(2,1)S(1)}, u32[]{:S(2)}, u32[]{:S(2)}) collective-permute-start(bf16[4,1040,128]{2,1,0:T(8,128)(2,1)S(1)} %get-tuple-element.17), channel_id=1, source_target_pairs={{0,1},{1,0},{2,3},{3,2},{4,5},{5,4},{6,7},{7,6},{8,9},{9,8},{10,11... | collective-permute-start | bytes 3194888 | tf_op jit(solution)/shard_map/ppermute | solution.py:302
  8.9 2.6 %collective-permute-done.other_ref = bf16[4,1040,128]{2,1,0:T(8,128)(2,1)S(1)} collective-permute-done((bf16[4,1040,128]{2,1,0:T(8,128)(2,1)S(1)}, bf16[4,1040,128]{2,1,0:T(8,128)(2,1)S(1)}, u32[]{:S(2)}, u32[]{:S(2)}) %collective-permute-start) | collective-permute-done | bytes 1064992 | tf_op jit(solution)/shard_map/ppermute | solution.py:302
  11.5 0.5 join_cores.1
  12.1 0.0 copy-start
  12.1 5.1 %collective-permute-start.1 = (bf16[1040,128]{1,0:T(8,128)(2,1)S(1)}, bf16[1040,128]{1,0:T(8,128)(2,1)S(1)}, u32[]{:S(2)}, u32[]{:S(2)}) collective-permute-start(bf16[1040,128]{1,0:T(8,128)(2,1)S(1)} %get-tuple-element.19), channel_id=1, source_target_pairs={{0,16},{1,17},{2,18},{3,19},{4,20},{5,21},{6,22},{7,23},{8,24},{9,... | collective-permute-start | bytes 798728 | tf_op jit(solution)/shard_map/ppermute | solution.py:302
  17.2 2.6 %collective-permute-start.2 = (bf16[1040,128]{1,0:T(8,128)(2,1)S(1)}, bf16[1040,128]{1,0:T(8,128)(2,1)S(1)}, u32[]{:S(2)}, u32[]{:S(2)}) collective-permute-start(bf16[1040,128]{1,0:T(8,128)(2,1)S(1)} %get-tuple-element.20), channel_id=1, source_target_pairs={{0,8},{1,9},{2,10},{3,11},{4,12},{5,13},{6,14},{7,15},{8,16},{9,17... | collective-permute-start | bytes 798728 | tf_op jit(solution)/shard_map/ppermute | solution.py:302
  19.8 4.5 %collective-permute-start.3 = (bf16[1040,128]{1,0:T(8,128)(2,1)S(1)}, bf16[1040,128]{1,0:T(8,128)(2,1)S(1)}, u32[]{:S(2)}, u32[]{:S(2)}) collective-permute-start(bf16[1040,128]{1,0:T(8,128)(2,1)S(1)} %get-tuple-element.21), channel_id=1, source_target_pairs={{0,24},{1,25},{2,26},{3,27},{4,28},{5,29},{6,30},{7,31},{8,0},{9,1... | collective-permute-start | bytes 798728 | tf_op jit(solution)/shard_map/ppermute | solution.py:302
  24.3 0.5 collective-permute-done.1.in1
  24.7 4.9 %collective-permute-done.2.in2 = bf16[1040,128]{1,0:T(8,128)(2,1)S(1)} collective-permute-done((bf16[1040,128]{1,0:T(8,128)(2,1)S(1)}, bf16[1040,128]{1,0:T(8,128)(2,1)S(1)}, u32[]{:S(2)}, u32[]{:S(2)}) %collective-permute-start.2) | collective-permute-done | bytes 266272 | tf_op jit(solution)/shard_map/ppermute | solution.py:302
  29.6 0.3 collective-permute-done.3.in3
  30.0 0.3 join_y.1
  30.3 15.7 %collective-permute-start.4 = (bf16[272,128]{1,0:T(8,128)(2,1)S(1)}, bf16[272,128]{1,0:T(8,128)(2,1)S(1)}, u32[]{:S(2)}, u32[]{:S(2)}) collective-permute-start(bf16[272,128]{1,0:T(8,128)(2,1)S(1)} %get-tuple-element.23), channel_id=1, source_target_pairs={{0,4},{1,5},{2,6},{3,7},{4,0},{5,1},{6,2},{7,3},{8,12},{9,13},{10,... | collective-permute-start | bytes 208904 | tf_op jit(solution)/shard_map/ppermute | solution.py:302
  46.0 4.3 %collective-permute-start.5 = (bf16[272,128]{1,0:T(8,128)(2,1)S(1)}, bf16[272,128]{1,0:T(8,128)(2,1)S(1)}, u32[]{:S(2)}, u32[]{:S(2)}) collective-permute-start(bf16[272,128]{1,0:T(8,128)(2,1)S(1)} %get-tuple-element.24), channel_id=1, source_target_pairs={{0,2},{1,3},{2,4},{3,5},{4,6},{5,7},{6,0},{7,1},{8,10},{9,11},{10,... | collective-permute-start | bytes 208904 | tf_op jit(solution)/shard_map/ppermute | solution.py:302
  50.3 5.5 %collective-permute-start.6 = (bf16[272,128]{1,0:T(8,128)(2,1)S(1)}, bf16[272,128]{1,0:T(8,128)(2,1)S(1)}, u32[]{:S(2)}, u32[]{:S(2)}) collective-permute-start(bf16[272,128]{1,0:T(8,128)(2,1)S(1)} %get-tuple-element.25), channel_id=1, source_target_pairs={{0,6},{1,7},{2,0},{3,1},{4,2},{5,3},{6,4},{7,5},{8,14},{9,15},{10,... | collective-permute-start | bytes 208904 | tf_op jit(solution)/shard_map/ppermute | solution.py:302
  55.8 0.0 collective-permute-done.4.in1
  55.8 1.2 %collective-permute-done.5.in2 = bf16[272,128]{1,0:T(8,128)(2,1)S(1)} collective-permute-done((bf16[272,128]{1,0:T(8,128)(2,1)S(1)}, bf16[272,128]{1,0:T(8,128)(2,1)S(1)}, u32[]{:S(2)}, u32[]{:S(2)}) %collective-permute-start.5) | collective-permute-done | bytes 69664 | tf_op jit(solution)/shard_map/ppermute | solution.py:302
  57.0 6.5 %collective-permute-done.6.in3 = bf16[272,128]{1,0:T(8,128)(2,1)S(1)} collective-permute-done((bf16[272,128]{1,0:T(8,128)(2,1)S(1)}, bf16[272,128]{1,0:T(8,128)(2,1)S(1)}, u32[]{:S(2)}, u32[]{:S(2)}) %collective-permute-start.6) | collective-permute-done | bytes 69664 | tf_op jit(solution)/shard_map/ppermute | solution.py:302
  63.5 0.0 copy-done
  63.5 1.2 %join_z.1 = (f32[32,256]{1,0:T(8,128)}, f32[32,256]{1,0:T(8,128)}, f32[1,128]{1,0:T(1,128)}) custom-call(bf16[272,128]{1,0:T(8,128)(2,1)S(1)} %get-tuple-element.22.in0, bf16[272,128]{1,0:T(8,128)(2,1)S(1)} %collective-permute-done.4.in1, bf16[272,128]{1,0:T(8,128)(2,1)S(1)} %collective-permute-done.5.in2, bf16[272,128]{1,0:T(8,128)(2,1)S(1)} %collective-permute-done.6.in3, ...), custom_call_target="tpu_custom_call" | custom-call | tf_op jit(solution)/shard_map/join_z/pallas_call | solution.py:241
Async XLA Ops:
  6.9 4.6 %collective-permute-start = (bf16[4,1040,128]{2,1,0:T(8,128)(2,1)S(1)}, bf16[4,1040,128]{2,1,0:T(8,128)(2,1)S(1)}, u32[]{:S(2)}, u32[]{:S(2)}) collective-permute-start(bf16[4,1040,128]{2,1,0:T(8,128)(2,1)S(1)} %get-tuple-element.17), channel_id=1, source_target_pairs={{0,1},{1,0},{2,3},{3,2},{4,5},{5,4},{6,7},{7,6},{8,9},{9,8},{10,11... | collective-permute-start | bytes 3194888 | tf_op jit(solution)/shard_map/ppermute | solution.py:302
  12.1 51.5 %copy-start = (f32[2]{0:T(128)S(1)}, f32[2]{0:T(128)}, u32[]{:S(2)}) copy-start(f32[2]{0:T(128)} %target_ref.1) | copy-start | bytes 28
  12.1 12.6 %collective-permute-start.1 = (bf16[1040,128]{1,0:T(8,128)(2,1)S(1)}, bf16[1040,128]{1,0:T(8,128)(2,1)S(1)}, u32[]{:S(2)}, u32[]{:S(2)}) collective-permute-start(bf16[1040,128]{1,0:T(8,128)(2,1)S(1)} %get-tuple-element.19), channel_id=1, source_target_pairs={{0,16},{1,17},{2,18},{3,19},{4,20},{5,21},{6,22},{7,23},{8,24},{9,... | collective-permute-start | bytes 798728 | tf_op jit(solution)/shard_map/ppermute | solution.py:302
  17.2 12.4 %collective-permute-start.2 = (bf16[1040,128]{1,0:T(8,128)(2,1)S(1)}, bf16[1040,128]{1,0:T(8,128)(2,1)S(1)}, u32[]{:S(2)}, u32[]{:S(2)}) collective-permute-start(bf16[1040,128]{1,0:T(8,128)(2,1)S(1)} %get-tuple-element.20), channel_id=1, source_target_pairs={{0,8},{1,9},{2,10},{3,11},{4,12},{5,13},{6,14},{7,15},{8,16},{9,17... | collective-permute-start | bytes 798728 | tf_op jit(solution)/shard_map/ppermute | solution.py:302
  19.8 10.2 %collective-permute-start.3 = (bf16[1040,128]{1,0:T(8,128)(2,1)S(1)}, bf16[1040,128]{1,0:T(8,128)(2,1)S(1)}, u32[]{:S(2)}, u32[]{:S(2)}) collective-permute-start(bf16[1040,128]{1,0:T(8,128)(2,1)S(1)} %get-tuple-element.21), channel_id=1, source_target_pairs={{0,24},{1,25},{2,26},{3,27},{4,28},{5,29},{6,30},{7,31},{8,0},{9,1... | collective-permute-start | bytes 798728 | tf_op jit(solution)/shard_map/ppermute | solution.py:302
  30.3 25.5 %collective-permute-start.4 = (bf16[272,128]{1,0:T(8,128)(2,1)S(1)}, bf16[272,128]{1,0:T(8,128)(2,1)S(1)}, u32[]{:S(2)}, u32[]{:S(2)}) collective-permute-start(bf16[272,128]{1,0:T(8,128)(2,1)S(1)} %get-tuple-element.23), channel_id=1, source_target_pairs={{0,4},{1,5},{2,6},{3,7},{4,0},{5,1},{6,2},{7,3},{8,12},{9,13},{10,... | collective-permute-start | bytes 208904 | tf_op jit(solution)/shard_map/ppermute | solution.py:302
  46.0 11.0 %collective-permute-start.5 = (bf16[272,128]{1,0:T(8,128)(2,1)S(1)}, bf16[272,128]{1,0:T(8,128)(2,1)S(1)}, u32[]{:S(2)}, u32[]{:S(2)}) collective-permute-start(bf16[272,128]{1,0:T(8,128)(2,1)S(1)} %get-tuple-element.24), channel_id=1, source_target_pairs={{0,2},{1,3},{2,4},{3,5},{4,6},{5,7},{6,0},{7,1},{8,10},{9,11},{10,... | collective-permute-start | bytes 208904 | tf_op jit(solution)/shard_map/ppermute | solution.py:302
  50.3 13.2 %collective-permute-start.6 = (bf16[272,128]{1,0:T(8,128)(2,1)S(1)}, bf16[272,128]{1,0:T(8,128)(2,1)S(1)}, u32[]{:S(2)}, u32[]{:S(2)}) collective-permute-start(bf16[272,128]{1,0:T(8,128)(2,1)S(1)} %get-tuple-element.25), channel_id=1, source_target_pairs={{0,6},{1,7},{2,0},{3,1},{4,2},{5,3},{6,4},{7,5},{8,14},{9,15},{10,... | collective-permute-start | bytes 208904 | tf_op jit(solution)/shard_map/ppermute | solution.py:302

commit v3 on v2

--- a/solution.py
+++ b/solution.py
@@ -201,7 +201,7 @@
     note = note_rows(total, mean0, mean1)
     here = lax.rem(lax.div(lax.axis_index("tile"), NC), NZ)
     for away, out_ref in enumerate(out_refs):
-        z = lax.rem(here + away, NZ)
+        z = lax.bitwise_xor(here, away)
         part = pl.ds(pl.multiple_of(z * PART, PART), PART)
         a, b = merge([r[part, :] for r in in_refs], shares, offsets)
         out_ref[:HALF, :] = a
@@ -301,13 +301,16 @@
         ]
         return lax.ppermute(x, "tile", pairs)
 
+    def swap(x, dy, dz):
+        return lax.ppermute(x, "tile", [(place(y, z, c), place(y ^ dy, z ^ dz, c)) for y, z, c in everyone])
+
     other = move(send, 0, 0, 1)
     piece = jax.ShapeDtypeStruct((TAIL + NOTE, 128), BF16)
     pieces = call(core_kernel, (piece,) * NY, vmem(2), (keep, other), "join_cores")
     across = [move(pieces[2], 2, 0, 0), move(pieces[1], 1, 0, 0), move(pieces[3], 3, 0, 0)]
     piece = jax.ShapeDtypeStruct((PART + NOTE, 128), BF16)
     pieces = call(y_kernel, (piece,) * NZ, vmem(NY), (pieces[0], *across), "join_y")
-    across = [move(pieces[2], 0, 2, 0), move(pieces[1], 0, 1, 0), move(pieces[3], 0, 3, 0)]
+    across = [swap(pieces[2], 0, 2), swap(pieces[3], 0, 3), swap(pieces[1], 0, 1)]
     count = float(lax.axis_size("tile") * slots // 2)
     out = jax.ShapeDtypeStruct((ROWS, hid), F32)
     grad_w1, grad_w2, loss = call(

time: 65 us -> 62.5 us (0.962)
  starting transfers between devices: 39.6 us -> 36 us
  waiting for transfers between devices: 16.1 us -> 16.9 us
    ppermute x7 -> x4, starting transfers between devices: 39.6 us -> 14.1 us  [move(): return lax.ppermute(x, 'tile', pairs)]
    ppermute x0 -> x3, starting transfers between devices: none -> 21.9 us  [swap(): lax.ppermute(x, 'tile', [(place(y, z, c), place(y ^ dy, z ^ dz, c)) for y...]
    ppermute x0 -> x3, waiting for transfers between devices: none -> 8.56 us  [swap(): lax.ppermute(x, 'tile', [(place(y, z, c), place(y ^ dy, z ^ dz, c)) for y...]
    ppermute x7 -> x4, waiting for transfers between devices: 16.1 us -> 8.35 us  [move(): return lax.ppermute(x, 'tile', pairs)]
where the time goes in v3:
time: 62.5 us; the launch traced here: 62 us
  starting transfers between devices  36 us (58%)
  waiting for transfers between devices  16.9 us (27%)
  Pallas kernels  7.75 us (12%)
  between operations  1.37 us (2%)
    ppermute x3, starting transfers between devices, swap(): lax.ppermute(x, 'tile', [(place(y, z, c), place(y ^ dy, z ^ dz, c)) for y...  21.9 us
    ppermute x4, starting transfers between devices, move(): return lax.ppermute(x, 'tile', pairs)  14.1 us
    ppermute x3, waiting for transfers between devices, swap(): lax.ppermute(x, 'tile', [(place(y, z, c), place(y ^ dy, z ^ dz, c)) for y...  8.56 us
    ppermute x4, waiting for transfers between devices, move(): return lax.ppermute(x, 'tile', pairs)  8.35 us
    pallas_call x4, Pallas kernels, call(): pl.pallas_call(kernel, out_shape=out_shape, in_specs=in_specs, out_specs=...  7.75 us
  transfers between devices with their start and end apart: 7, of which 6 were waited for; matrix products, arithmetic and copies ran while one was open for 0% of the time, Pallas kernels for 0%

profile of v3, /device:TPU:6, one launch (start us, length us, event | category | flops | bytes accessed | tf_op | source)
XLA Modules:
  0.0 62.0 jit_solution(10991317024384341754)
XLA Ops:
  1.3 5.6 %local.1 = (bf16[4,1040,128]{2,1,0:T(8,128)(2,1)S(1)}, bf16[4,1040,128]{2,1,0:T(8,128)(2,1)S(1)}) custom-call(s32[1]{0:T(128)S(6)} %copy.12.count_ref, bf16[1024,1024]{1,0:T(8,128)(2,1)} %bitcast.5, bf16[1024,256]{1,0:T(8,128)(2,1)} %w_reduce_hbm.1, bf16[1024,256]{1,0:T(8,128)(2,1)} %w_expand_hbm.1, bf16[1024,256]{1,0:T(8,128)(2,1)} %att_tanh_hbm.1, ...), custom_call_target="tpu_custom_call" | custom-call | tf_op jit(solution)/shard_map/local/pallas_call | solution.py:241
  6.9 1.9 %collective-permute-start = (bf16[4,1040,128]{2,1,0:T(8,128)(2,1)S(1)}, bf16[4,1040,128]{2,1,0:T(8,128)(2,1)S(1)}, u32[]{:S(2)}, u32[]{:S(2)}) collective-permute-start(bf16[4,1040,128]{2,1,0:T(8,128)(2,1)S(1)} %get-tuple-element.17), channel_id=1, source_target_pairs={{0,1},{1,0},{2,3},{3,2},{4,5},{5,4},{6,7},{7,6},{8,9},{9,8},{10,11... | collective-permute-start | bytes 3194888 | tf_op jit(solution)/shard_map/ppermute | solution.py:302
  8.9 2.6 %collective-permute-done.other_ref = bf16[4,1040,128]{2,1,0:T(8,128)(2,1)S(1)} collective-permute-done((bf16[4,1040,128]{2,1,0:T(8,128)(2,1)S(1)}, bf16[4,1040,128]{2,1,0:T(8,128)(2,1)S(1)}, u32[]{:S(2)}, u32[]{:S(2)}) %collective-permute-start) | collective-permute-done | bytes 1064992 | tf_op jit(solution)/shard_map/ppermute | solution.py:302
  11.5 0.5 join_cores.1
  12.1 0.0 copy-start
  12.1 5.1 %collective-permute-start.1 = (bf16[1040,128]{1,0:T(8,128)(2,1)S(1)}, bf16[1040,128]{1,0:T(8,128)(2,1)S(1)}, u32[]{:S(2)}, u32[]{:S(2)}) collective-permute-start(bf16[1040,128]{1,0:T(8,128)(2,1)S(1)} %get-tuple-element.19), channel_id=1, source_target_pairs={{0,16},{1,17},{2,18},{3,19},{4,20},{5,21},{6,22},{7,23},{8,24},{9,... | collective-permute-start | bytes 798728 | tf_op jit(solution)/shard_map/ppermute | solution.py:302
  17.2 2.6 %collective-permute-start.2 = (bf16[1040,128]{1,0:T(8,128)(2,1)S(1)}, bf16[1040,128]{1,0:T(8,128)(2,1)S(1)}, u32[]{:S(2)}, u32[]{:S(2)}) collective-permute-start(bf16[1040,128]{1,0:T(8,128)(2,1)S(1)} %get-tuple-element.20), channel_id=1, source_target_pairs={{0,8},{1,9},{2,10},{3,11},{4,12},{5,13},{6,14},{7,15},{8,16},{9,17... | collective-permute-start | bytes 798728 | tf_op jit(solution)/shard_map/ppermute | solution.py:302
  19.8 4.5 %collective-permute-start.3 = (bf16[1040,128]{1,0:T(8,128)(2,1)S(1)}, bf16[1040,128]{1,0:T(8,128)(2,1)S(1)}, u32[]{:S(2)}, u32[]{:S(2)}) collective-permute-start(bf16[1040,128]{1,0:T(8,128)(2,1)S(1)} %get-tuple-element.21), channel_id=1, source_target_pairs={{0,24},{1,25},{2,26},{3,27},{4,28},{5,29},{6,30},{7,31},{8,0},{9,1... | collective-permute-start | bytes 798728 | tf_op jit(solution)/shard_map/ppermute | solution.py:302
  24.3 0.5 collective-permute-done.1.in1
  24.7 4.9 %collective-permute-done.2.in2 = bf16[1040,128]{1,0:T(8,128)(2,1)S(1)} collective-permute-done((bf16[1040,128]{1,0:T(8,128)(2,1)S(1)}, bf16[1040,128]{1,0:T(8,128)(2,1)S(1)}, u32[]{:S(2)}, u32[]{:S(2)}) %collective-permute-start.2) | collective-permute-done | bytes 266272 | tf_op jit(solution)/shard_map/ppermute | solution.py:302
  29.6 0.3 collective-permute-done.3.in3
  30.0 0.3 join_y.1
  30.3 15.7 %collective-permute-start.4 = (bf16[272,128]{1,0:T(8,128)(2,1)S(1)}, bf16[272,128]{1,0:T(8,128)(2,1)S(1)}, u32[]{:S(2)}, u32[]{:S(2)}) collective-permute-start(bf16[272,128]{1,0:T(8,128)(2,1)S(1)} %get-tuple-element.23), channel_id=1, source_target_pairs={{0,4},{1,5},{2,6},{3,7},{4,0},{5,1},{6,2},{7,3},{8,12},{9,13},{10,... | collective-permute-start | bytes 208904 | tf_op jit(solution)/shard_map/ppermute | solution.py:305
  46.0 1.9 %collective-permute-start.5 = (bf16[272,128]{1,0:T(8,128)(2,1)S(1)}, bf16[272,128]{1,0:T(8,128)(2,1)S(1)}, u32[]{:S(2)}, u32[]{:S(2)}) collective-permute-start(bf16[272,128]{1,0:T(8,128)(2,1)S(1)} %get-tuple-element.24), channel_id=1, source_target_pairs={{0,6},{1,7},{2,4},{3,5},{4,2},{5,3},{6,0},{7,1},{8,14},{9,15},{10,... | collective-permute-start | bytes 208904 | tf_op jit(solution)/shard_map/ppermute | solution.py:305
  47.9 4.3 %collective-permute-start.6 = (bf16[272,128]{1,0:T(8,128)(2,1)S(1)}, bf16[272,128]{1,0:T(8,128)(2,1)S(1)}, u32[]{:S(2)}, u32[]{:S(2)}) collective-permute-start(bf16[272,128]{1,0:T(8,128)(2,1)S(1)} %get-tuple-element.25), channel_id=1, source_target_pairs={{0,2},{1,3},{2,0},{3,1},{4,6},{5,7},{6,4},{7,5},{8,10},{9,11},{10,... | collective-permute-start | bytes 208904 | tf_op jit(solution)/shard_map/ppermute | solution.py:305
  52.2 0.0 collective-permute-done.4.in1
  52.2 5.9 %collective-permute-done.5.in2 = bf16[272,128]{1,0:T(8,128)(2,1)S(1)} collective-permute-done((bf16[272,128]{1,0:T(8,128)(2,1)S(1)}, bf16[272,128]{1,0:T(8,128)(2,1)S(1)}, u32[]{:S(2)}, u32[]{:S(2)}) %collective-permute-start.5) | collective-permute-done | bytes 69664 | tf_op jit(solution)/shard_map/ppermute | solution.py:305
  58.1 2.7 %collective-permute-done.6.in3 = bf16[272,128]{1,0:T(8,128)(2,1)S(1)} collective-permute-done((bf16[272,128]{1,0:T(8,128)(2,1)S(1)}, bf16[272,128]{1,0:T(8,128)(2,1)S(1)}, u32[]{:S(2)}, u32[]{:S(2)}) %collective-permute-start.6) | collective-permute-done | bytes 69664 | tf_op jit(solution)/shard_map/ppermute | solution.py:305
  60.8 0.0 copy-done
  60.8 1.2 %join_z.1 = (f32[32,256]{1,0:T(8,128)}, f32[32,256]{1,0:T(8,128)}, f32[1,128]{1,0:T(1,128)}) custom-call(bf16[272,128]{1,0:T(8,128)(2,1)S(1)} %get-tuple-element.22.in0, bf16[272,128]{1,0:T(8,128)(2,1)S(1)} %collective-permute-done.4.in1, bf16[272,128]{1,0:T(8,128)(2,1)S(1)} %collective-permute-done.5.in2, bf16[272,128]{1,0:T(8,128)(2,1)S(1)} %collective-permute-done.6.in3, ...), custom_call_target="tpu_custom_call" | custom-call | tf_op jit(solution)/shard_map/join_z/pallas_call | solution.py:241
Async XLA Ops:
  6.9 4.6 %collective-permute-start = (bf16[4,1040,128]{2,1,0:T(8,128)(2,1)S(1)}, bf16[4,1040,128]{2,1,0:T(8,128)(2,1)S(1)}, u32[]{:S(2)}, u32[]{:S(2)}) collective-permute-start(bf16[4,1040,128]{2,1,0:T(8,128)(2,1)S(1)} %get-tuple-element.17), channel_id=1, source_target_pairs={{0,1},{1,0},{2,3},{3,2},{4,5},{5,4},{6,7},{7,6},{8,9},{9,8},{10,11... | collective-permute-start | bytes 3194888 | tf_op jit(solution)/shard_map/ppermute | solution.py:302
  12.1 48.7 %copy-start = (f32[2]{0:T(128)S(1)}, f32[2]{0:T(128)}, u32[]{:S(2)}) copy-start(f32[2]{0:T(128)} %target_ref.1) | copy-start | bytes 28
  12.1 12.6 %collective-permute-start.1 = (bf16[1040,128]{1,0:T(8,128)(2,1)S(1)}, bf16[1040,128]{1,0:T(8,128)(2,1)S(1)}, u32[]{:S(2)}, u32[]{:S(2)}) collective-permute-start(bf16[1040,128]{1,0:T(8,128)(2,1)S(1)} %get-tuple-element.19), channel_id=1, source_target_pairs={{0,16},{1,17},{2,18},{3,19},{4,20},{5,21},{6,22},{7,23},{8,24},{9,... | collective-permute-start | bytes 798728 | tf_op jit(solution)/shard_map/ppermute | solution.py:302
  17.2 12.4 %collective-permute-start.2 = (bf16[1040,128]{1,0:T(8,128)(2,1)S(1)}, bf16[1040,128]{1,0:T(8,128)(2,1)S(1)}, u32[]{:S(2)}, u32[]{:S(2)}) collective-permute-start(bf16[1040,128]{1,0:T(8,128)(2,1)S(1)} %get-tuple-element.20), channel_id=1, source_target_pairs={{0,8},{1,9},{2,10},{3,11},{4,12},{5,13},{6,14},{7,15},{8,16},{9,17... | collective-permute-start | bytes 798728 | tf_op jit(solution)/shard_map/ppermute | solution.py:302
  19.8 10.2 %collective-permute-start.3 = (bf16[1040,128]{1,0:T(8,128)(2,1)S(1)}, bf16[1040,128]{1,0:T(8,128)(2,1)S(1)}, u32[]{:S(2)}, u32[]{:S(2)}) collective-permute-start(bf16[1040,128]{1,0:T(8,128)(2,1)S(1)} %get-tuple-element.21), channel_id=1, source_target_pairs={{0,24},{1,25},{2,26},{3,27},{4,28},{5,29},{6,30},{7,31},{8,0},{9,1... | collective-permute-start | bytes 798728 | tf_op jit(solution)/shard_map/ppermute | solution.py:302
  30.3 22.0 %collective-permute-start.4 = (bf16[272,128]{1,0:T(8,128)(2,1)S(1)}, bf16[272,128]{1,0:T(8,128)(2,1)S(1)}, u32[]{:S(2)}, u32[]{:S(2)}) collective-permute-start(bf16[272,128]{1,0:T(8,128)(2,1)S(1)} %get-tuple-element.23), channel_id=1, source_target_pairs={{0,4},{1,5},{2,6},{3,7},{4,0},{5,1},{6,2},{7,3},{8,12},{9,13},{10,... | collective-permute-start | bytes 208904 | tf_op jit(solution)/shard_map/ppermute | solution.py:305
  46.0 12.1 %collective-permute-start.5 = (bf16[272,128]{1,0:T(8,128)(2,1)S(1)}, bf16[272,128]{1,0:T(8,128)(2,1)S(1)}, u32[]{:S(2)}, u32[]{:S(2)}) collective-permute-start(bf16[272,128]{1,0:T(8,128)(2,1)S(1)} %get-tuple-element.24), channel_id=1, source_target_pairs={{0,6},{1,7},{2,4},{3,5},{4,2},{5,3},{6,0},{7,1},{8,14},{9,15},{10,... | collective-permute-start | bytes 208904 | tf_op jit(solution)/shard_map/ppermute | solution.py:305
  47.9 12.9 %collective-permute-start.6 = (bf16[272,128]{1,0:T(8,128)(2,1)S(1)}, bf16[272,128]{1,0:T(8,128)(2,1)S(1)}, u32[]{:S(2)}, u32[]{:S(2)}) collective-permute-start(bf16[272,128]{1,0:T(8,128)(2,1)S(1)} %get-tuple-element.25), channel_id=1, source_target_pairs={{0,2},{1,3},{2,0},{3,1},{4,6},{5,7},{6,4},{7,5},{8,10},{9,11},{10,... | collective-permute-start | bytes 208904 | tf_op jit(solution)/shard_map/ppermute | solution.py:305

commit v4 on v3

--- a/solution.py
+++ b/solution.py
@@ -13,7 +13,15 @@
 ROWS = 32
 PART = 8 * ROWS
 HALF = PART // 2
-TAIL = NZ * PART
+W1_PART = 4 * ROWS
+W1_ROWS = NZ * W1_PART
+PATH_ROWS = NZ * ROWS
+SLOTS = 64
+CORE_PATH = NY * W1_ROWS
+CORE_SUMS = CORE_PATH + NY * PATH_ROWS
+CORE_NOTE = CORE_SUMS + 2 * SLOTS
+Y_SUMS = W1_ROWS + PATH_ROWS
+Y_NOTE = Y_SUMS + 4 * SLOTS
 NOTE = 16
 VMEM_LIMIT = 48 * 1024 * 1024
 
@@ -30,15 +38,18 @@
     return [high.astype(F32), mid.astype(F32), low.astype(F32)]
 
 
-def note_rows(total, mean0, mean1):
-    rows = split3(total) + split3(mean0) + split3(mean1)
-    rows.append(jnp.zeros((NOTE - len(rows), rows[0].shape[1]), F32))
+def note_rows(*values):
+    rows = [part for value in values for part in split3(value)]
+    if len(rows) < NOTE:
+        rows.append(jnp.zeros((NOTE - len(rows), rows[0].shape[1]), F32))
     return jnp.concatenate(rows, axis=0).astype(BF16)
 
 
-def read_note(note):
+def read_note(note, count):
     rows = note.astype(F32)
-    return [rows[i : i + 1] + rows[i + 1 : i + 2] + rows[i + 2 : i + 3] for i in (0, 3, 6)]
+    return [
+        rows[i : i + 1] + rows[i + 1 : i + 2] + rows[i + 2 : i + 3] for i in range(0, 3 * count, 3)
+    ]
 
 
 def merge_notes(notes):
@@ -54,7 +65,7 @@
     return jnp.sum(x.reshape(x.shape[0] // 16, 16, x.shape[1]).astype(F32), axis=1)
 
 
-def store_parts(part_a, part_b, which, keep_ref, send_ref):
+def store_w1(part_a, part_b, keep_ref, send_ref):
     first = lax.rem(lax.axis_index("tile"), NC) == 0
     for y in range(NY):
         for z in range(NZ):
@@ -64,9 +75,25 @@
                     cols = slice(half * 128, half * 128 + 128)
                     even = part[at : at + ROWS, cols].astype(BF16)
                     odd = part[at + ROWS : at + 2 * ROWS, cols].astype(BF16)
-                    here = pl.ds(z * PART + (4 * i + 2 * which + half) * ROWS, ROWS)
-                    keep_ref[y, here, :] = jnp.where(first, even, odd)
-                    send_ref[y, here, :] = jnp.where(first, odd, even)
+                    here = pl.ds(y * W1_ROWS + z * W1_PART + (2 * i + half) * ROWS, ROWS)
+                    keep_ref[here, :] = jnp.where(first, even, odd)
+                    send_ref[here, :] = jnp.where(first, odd, even)
+
+
+def store_path(path, keep_ref, send_ref):
+    first = lax.rem(lax.axis_index("tile"), NC) == 0
+    for k in range(NY * NZ):
+        at = k * NC * ROWS
+        even, odd = path[at : at + ROWS], path[at + ROWS : at + 2 * ROWS]
+        here = pl.ds(CORE_PATH + k * ROWS, ROWS)
+        keep_ref[here, :] = jnp.where(first, even[:, :128], odd[:, :128]).astype(BF16)
+        send_ref[here, :] = jnp.where(first, odd[:, 128:], even[:, 128:]).astype(BF16)
+
+
+def as_row(column, shift):
+    slot = lax.broadcasted_iota(jnp.int32, (column.shape[0], 128), 0)
+    lane = lax.broadcasted_iota(jnp.int32, (column.shape[0], 128), 1)
+    return jnp.sum(jnp.where(slot + shift == lane, column, 0.0), axis=0, keepdims=True)
 
 
 CHUNKS = 2
@@ -150,13 +177,16 @@
     path = dot(e_tanh, att_tanh, ((1,), (1,))) + dot(e_gate, att_gate, ((1,), (1,)))
     dy_a = ((share * (class0 - class1) + slope * path) * (1.0 / 16.0)).astype(BF16)
     dy_b = (share * path * (1.0 / 16.0)).astype(BF16)
-    w2_a = dot(jnp.concatenate([dy_a, dy_a], axis=0), sums, ((0,), (0,)))
-    w2_b = dot(jnp.concatenate([dy_b, dy_b], axis=0), sums, ((0,), (0,)))
-    store_parts(w2_a, w2_b, 1, keep_ref, send_ref)
-    note = note_rows(*[jnp.broadcast_to(v, (1, 128)) for v in (total, mean0, mean1)])
-    for y in range(NY):
-        keep_ref[y, TAIL:, :] = note
-        send_ref[y, TAIL:, :] = note
+    blank = jnp.zeros((2 * slots, e_tanh.shape[1]), BF16)
+    path_t = dot(att_tanh, jnp.concatenate([e_tanh, blank, e_tanh], axis=0), ((1,), (1,))) + dot(
+        att_gate, jnp.concatenate([e_gate, blank, e_gate], axis=0), ((1,), (1,))
+    )
+    store_path(path_t, keep_ref, send_ref)
+    scalars = [jnp.broadcast_to(v, (1, 128)) for v in (total, mean0, mean1)]
+    for out_ref, shift in ((keep_ref, 0), (send_ref, slots)):
+        out_ref[CORE_SUMS : CORE_SUMS + slots, :] = sum_high[:, :128]
+        out_ref[CORE_SUMS + slots : CORE_NOTE, :] = sum_high[:, 128:]
+        out_ref[CORE_NOTE:, :] = note_rows(*scalars, as_row(share, shift), as_row(u0 - u1, shift))
     back = dot(jnp.concatenate([dy_a, dy_b], axis=0), w_expand, ((1,), (0,))).astype(BF16)
     back = jnp.concatenate([back[:slots], back[slots:]], axis=1)
     spread = jnp.broadcast_to(back.astype(F32)[:, None, :], (slots, 16, back.shape[1]))
@@ -167,51 +197,87 @@
         [jnp.where(mask, spread[:, :hid], 0.0), jnp.where(mask, spread[:, hid:], 0.0)], axis=1
     ).astype(BF16)
     grad_w1 = dot(flat_ref[...], dhid, ((0,), (0,)))
-    store_parts(grad_w1[:, :hid], grad_w1[:, hid:], 0, keep_ref, send_ref)
+    store_w1(grad_w1[:, :hid], grad_w1[:, hid:], keep_ref, send_ref)
 
 
 def merge(blocks, shares, offsets):
     a = b = 0.0
+    half = blocks[0].shape[0] // 2
     for share, offset, block in zip(shares, offsets, blocks):
-        block_b = block[HALF:].astype(F32)
-        a = a + share * (block[:HALF].astype(F32) + offset * block_b)
+        block_b = block[half:].astype(F32)
+        a = a + share * (block[:half].astype(F32) + offset * block_b)
         b = b + share * block_b
     return a.astype(BF16), b.astype(BF16)
 
 
 def core_kernel(own_ref, other_ref, *out_refs):
-    notes = [read_note(r[0, TAIL:, :]) for r in (own_ref, other_ref)]
+    in_refs = (own_ref, other_ref)
+    notes = [read_note(r[CORE_NOTE:, :], 5) for r in in_refs]
     total, mean0, mean1, shares, offsets = merge_notes(notes)
-    note = note_rows(total, mean0, mean1)
+    tile_share = shares[0] * notes[0][3] + shares[1] * notes[1][3]
+    note = note_rows(total, mean0, mean1, tile_share, notes[0][4] + notes[1][4])
     here = lax.div(lax.axis_index("tile"), NZ * NC)
     for away, out_ref in enumerate(out_refs):
         y = lax.rem(here + away, NY)
         for z in range(NZ):
-            part = slice(z * PART, (z + 1) * PART)
-            a, b = merge([r[y, part, :] for r in (own_ref, other_ref)], shares, offsets)
-            out_ref[z * PART : z * PART + HALF, :] = a
-            out_ref[z * PART + HALF : (z + 1) * PART, :] = b
-        out_ref[TAIL:, :] = note
-
-
-def y_kernel(in0, in1, in2, in3, *out_refs):
-    in_refs = (in0, in1, in2, in3)
-    notes = [read_note(r[TAIL:, :]) for r in in_refs]
+            part = pl.ds(pl.multiple_of(y * W1_ROWS + z * W1_PART, W1_PART), W1_PART)
+            a, b = merge([r[part, :] for r in in_refs], shares, offsets)
+            out_ref[z * W1_PART : z * W1_PART + W1_PART // 2, :] = a
+            out_ref[z * W1_PART + W1_PART // 2 : (z + 1) * W1_PART, :] = b
+        path = pl.ds(pl.multiple_of(CORE_PATH + y * PATH_ROWS, PATH_ROWS), PATH_ROWS)
+        out_ref[W1_ROWS:Y_SUMS, :] = own_ref[path, :] + other_ref[path, :]
+        for half in range(2):
+            for i, r in enumerate(in_refs):
+                at = Y_SUMS + (2 * half + i) * SLOTS
+                out_ref[at : at + SLOTS, :] = r[CORE_SUMS + half * SLOTS : CORE_SUMS + (half + 1) * SLOTS, :]
+        out_ref[Y_NOTE:, :] = note
+
+
+def class_column(classifier_ref, y, core):
+    span = NZ * NC * ROWS
+    part = pl.ds(pl.multiple_of(y * span, span), span)
+    row = classifier_ref[0:1, part] - classifier_ref[1:2, part]
+    rows = jnp.concatenate(split3(row) + [jnp.zeros((5, span), F32)], axis=0).astype(BF16)
+    to = lax.broadcasted_iota(jnp.int32, (PATH_ROWS, span), 0)
+    at = lax.broadcasted_iota(jnp.int32, (PATH_ROWS, span), 1)
+    wanted = lax.div(to, ROWS) * (NC * ROWS) + core * ROWS + lax.rem(to, ROWS)
+    picked = dot((wanted == at).astype(F32).astype(BF16), rows, ((1,), (1,)))
+    return picked[:, 0:1] + picked[:, 1:2] + picked[:, 2:3]
+
+
+def y_kernel(in0, in1, in2, in3, classifier_ref, *refs):
+    in_refs, out_refs, w2_ref = (in0, in1, in2, in3), refs[:-1], refs[-1]
+    notes = [read_note(r[Y_NOTE:, :], 5) for r in in_refs]
     total, mean0, mean1, shares, offsets = merge_notes(notes)
     note = note_rows(total, mean0, mean1)
-    here = lax.rem(lax.div(lax.axis_index("tile"), NC), NZ)
+    index = lax.axis_index("tile")
+    column = class_column(classifier_ref, lax.div(index, NZ * NC), lax.rem(index, NC))
+    lefts, sums = [], []
+    for share, member, r in zip(shares, notes, in_refs):
+        path = r[W1_ROWS:Y_SUMS, :].astype(F32)
+        weight = share * member[3] * (1.0 / 16.0)
+        slope = weight * (member[4] - (mean0 - mean1))
+        lefts.append(jnp.concatenate([weight * column + slope * path, weight * path], axis=0).astype(BF16))
+        halves = [r[Y_SUMS + 2 * i * SLOTS : Y_SUMS + 2 * (i + 1) * SLOTS, :] for i in range(2)]
+        sums.append(jnp.concatenate(halves, axis=1))
+    w2_ref[...] = dot(jnp.concatenate(lefts, axis=1), jnp.concatenate(sums, axis=0), ((1,), (0,))).astype(BF16)
+    here = lax.rem(lax.div(index, NC), NZ)
     for away, out_ref in enumerate(out_refs):
         z = lax.bitwise_xor(here, away)
-        part = pl.ds(pl.multiple_of(z * PART, PART), PART)
+        part = pl.ds(pl.multiple_of(z * W1_PART, W1_PART), W1_PART)
         a, b = merge([r[part, :] for r in in_refs], shares, offsets)
-        out_ref[:HALF, :] = a
-        out_ref[HALF:PART, :] = b
+        for i, block in enumerate((a, b)):
+            out_ref[i * HALF : i * HALF + HALF // 2, :] = block
+            rows = pl.ds(pl.multiple_of(i * PATH_ROWS + z * ROWS, ROWS), ROWS)
+            for half in range(2):
+                at = i * HALF + HALF // 2 + half * ROWS
+                out_ref[at : at + ROWS, :] = w2_ref[rows, half * 128 : half * 128 + 128]
         out_ref[PART:, :] = note
 
 
 def z_kernel(count, in0, in1, in2, in3, target_ref, w1_ref, w2_ref, loss_ref):
     in_refs = (in0, in1, in2, in3)
-    notes = [read_note(r[PART:, :]) for r in in_refs]
+    notes = [read_note(r[PART:, :], 3) for r in in_refs]
     total, mean0, mean1, shares, offsets = merge_notes(notes)
     width = mean0.shape[1]
     target0 = jnp.full((1, width), target_ref[0], F32)
@@ -281,7 +347,7 @@
             classifier.T,
         )
     ]
-    chunk = jax.ShapeDtypeStruct((NY, TAIL + NOTE, 128), BF16)
+    chunk = jax.ShapeDtypeStruct((CORE_NOTE + NOTE, 128), BF16)
     keep, send = call(
         local_kernel,
         (chunk, chunk),
@@ -305,11 +371,18 @@
         return lax.ppermute(x, "tile", [(place(y, z, c), place(y ^ dy, z ^ dz, c)) for y, z, c in everyone])
 
     other = move(send, 0, 0, 1)
-    piece = jax.ShapeDtypeStruct((TAIL + NOTE, 128), BF16)
+    piece = jax.ShapeDtypeStruct((Y_NOTE + NOTE, 128), BF16)
     pieces = call(core_kernel, (piece,) * NY, vmem(2), (keep, other), "join_cores")
     across = [move(pieces[2], 2, 0, 0), move(pieces[1], 1, 0, 0), move(pieces[3], 3, 0, 0)]
     piece = jax.ShapeDtypeStruct((PART + NOTE, 128), BF16)
-    pieces = call(y_kernel, (piece,) * NZ, vmem(NY), (pieces[0], *across), "join_y")
+    pieces = call(
+        y_kernel,
+        (piece,) * NZ,
+        vmem(NY + 1),
+        (pieces[0], *across, classifier.T),
+        "join_y",
+        [pltpu.VMEM((2 * PATH_ROWS, hid), BF16)],
+    )
     across = [swap(pieces[2], 0, 2), swap(pieces[3], 0, 3), swap(pieces[1], 0, 1)]
     count = float(lax.axis_size("tile") * slots // 2)
     out = jax.ShapeDtypeStruct((ROWS, hid), F32)

time: 62.5 us -> 61 us (0.976)
  waiting for transfers between devices: 16.9 us -> 15.2 us
    ppermute x4, waiting for transfers between devices: 8.35 us -> 6.78 us  [move(): return lax.ppermute(x, 'tile', pairs)]
  transfers between devices with their start and end apart: 7 -> 7, of which waited for: 6 -> 5; matrix products, arithmetic and copies ran while one was open for 0% -> 0% of each run, Pallas kernels for 0% -> 0%
where the time goes in v4:
time: 61 us; the launch traced here: 60.4 us
  starting transfers between devices  36 us (59%)
  waiting for transfers between devices  15.2 us (25%)
  Pallas kernels  7.82 us (13%)
  between operations  1.39 us (2%)
    ppermute x3, starting transfers between devices, swap(): lax.ppermute(x, 'tile', [(place(y, z, c), place(y ^ dy, z ^ dz, c)) for y...  21.9 us
    ppermute x4, starting transfers between devices, move(): return lax.ppermute(x, 'tile', pairs)  14.1 us
    ppermute x3, waiting for transfers between devices, swap(): lax.ppermute(x, 'tile', [(place(y, z, c), place(y ^ dy, z ^ dz, c)) for y...  8.39 us
    pallas_call x4, Pallas kernels, call(): pl.pallas_call(kernel, out_shape=out_shape, in_specs=in_specs, out_specs=...  7.82 us
    ppermute x4, waiting for transfers between devices, move(): return lax.ppermute(x, 'tile', pairs)  6.78 us
  transfers between devices with their start and end apart: 7, of which 5 were waited for; matrix products, arithmetic and copies ran while one was open for 0% of the time, Pallas kernels for 0%

profile of v4, /device:TPU:6, one launch (start us, length us, event | category | flops | bytes accessed | tf_op | source)
XLA Modules:
  0.0 60.4 jit_solution(12194305488100601232)
XLA Ops:
  1.3 0.0 copy-start
  1.3 5.6 %local.1 = (bf16[2704,128]{1,0:T(8,128)(2,1)S(1)}, bf16[2704,128]{1,0:T(8,128)(2,1)S(1)}) custom-call(s32[1]{0:T(128)S(6)} %copy.12.count_ref, bf16[1024,1024]{1,0:T(8,128)(2,1)} %bitcast.7, bf16[1024,256]{1,0:T(8,128)(2,1)} %w_reduce_hbm.1, bf16[1024,256]{1,0:T(8,128)(2,1)} %w_expand_hbm.1, bf16[1024,256]{1,0:T(8,128)(2,1)} %att_tanh_hbm.1, ...), custom_call_target="tpu_custom_call" | custom-call | tf_op jit(solution)/shard_map/local/pallas_call | solution.py:307
  6.9 0.0 copy-start.1
  6.9 1.9 %collective-permute-start = (bf16[2704,128]{1,0:T(8,128)(2,1)S(1)}, bf16[2704,128]{1,0:T(8,128)(2,1)S(1)}, u32[]{:S(2)}, u32[]{:S(2)}) collective-permute-start(bf16[2704,128]{1,0:T(8,128)(2,1)S(1)} %get-tuple-element.17), channel_id=1, source_target_pairs={{0,1},{1,0},{2,3},{3,2},{4,5},{5,4},{6,7},{7,6},{8,9},{9,8},{10,11... | collective-permute-start | bytes 2076680 | tf_op jit(solution)/shard_map/ppermute | solution.py:368
  8.8 2.1 %collective-permute-done.other_ref = bf16[2704,128]{1,0:T(8,128)(2,1)S(1)} collective-permute-done((bf16[2704,128]{1,0:T(8,128)(2,1)S(1)}, bf16[2704,128]{1,0:T(8,128)(2,1)S(1)}, u32[]{:S(2)}, u32[]{:S(2)}) %collective-permute-start) | collective-permute-done | bytes 692256 | tf_op jit(solution)/shard_map/ppermute | solution.py:368
  11.0 0.3 join_cores.1
  11.3 5.1 %collective-permute-start.1 = (bf16[912,128]{1,0:T(8,128)(2,1)S(1)}, bf16[912,128]{1,0:T(8,128)(2,1)S(1)}, u32[]{:S(2)}, u32[]{:S(2)}) collective-permute-start(bf16[912,128]{1,0:T(8,128)(2,1)S(1)} %get-tuple-element.19), channel_id=1, source_target_pairs={{0,16},{1,17},{2,18},{3,19},{4,20},{5,21},{6,22},{7,23},{8,24},{9,... | collective-permute-start | bytes 700424 | tf_op jit(solution)/shard_map/ppermute | solution.py:368
  16.4 2.6 %collective-permute-start.2 = (bf16[912,128]{1,0:T(8,128)(2,1)S(1)}, bf16[912,128]{1,0:T(8,128)(2,1)S(1)}, u32[]{:S(2)}, u32[]{:S(2)}) collective-permute-start(bf16[912,128]{1,0:T(8,128)(2,1)S(1)} %get-tuple-element.20), channel_id=1, source_target_pairs={{0,8},{1,9},{2,10},{3,11},{4,12},{5,13},{6,14},{7,15},{8,16},{9,17... | collective-permute-start | bytes 700424 | tf_op jit(solution)/shard_map/ppermute | solution.py:368
  19.0 4.5 %collective-permute-start.3 = (bf16[912,128]{1,0:T(8,128)(2,1)S(1)}, bf16[912,128]{1,0:T(8,128)(2,1)S(1)}, u32[]{:S(2)}, u32[]{:S(2)}) collective-permute-start(bf16[912,128]{1,0:T(8,128)(2,1)S(1)} %get-tuple-element.21), channel_id=1, source_target_pairs={{0,24},{1,25},{2,26},{3,27},{4,28},{5,29},{6,30},{7,31},{8,0},{9,1... | collective-permute-start | bytes 700424 | tf_op jit(solution)/shard_map/ppermute | solution.py:368
  23.4 0.0 collective-permute-done.1.in1
  23.5 4.1 %collective-permute-done.2.in2 = bf16[912,128]{1,0:T(8,128)(2,1)S(1)} collective-permute-done((bf16[912,128]{1,0:T(8,128)(2,1)S(1)}, bf16[912,128]{1,0:T(8,128)(2,1)S(1)}, u32[]{:S(2)}, u32[]{:S(2)}) %collective-permute-start.2) | collective-permute-done | bytes 233504 | tf_op jit(solution)/shard_map/ppermute | solution.py:368
  27.6 0.5 collective-permute-done.3.in3
  28.1 0.0 copy-done
  28.1 0.7 %join_y.1 = (bf16[272,128]{1,0:T(8,128)(2,1)S(1)}, bf16[272,128]{1,0:T(8,128)(2,1)S(1)}, bf16[272,128]{1,0:T(8,128)(2,1)S(1)}, bf16[272,128]{1,0:T(8,128)(2,1)S(1)}) custom-call(bf16[912,128]{1,0:T(8,128)(2,1)S(1)} %get-tuple-element.18.in0, bf16[912,128]{1,0:T(8,128)(2,1)S(1)} %collective-permute-done.1.in1, ...), custom_call_target="tpu_custom_call" | custom-call | tf_op jit(solution)/shard_map/join_y/pallas_call | solution.py:307
  28.8 15.7 %collective-permute-start.4 = (bf16[272,128]{1,0:T(8,128)(2,1)S(1)}, bf16[272,128]{1,0:T(8,128)(2,1)S(1)}, u32[]{:S(2)}, u32[]{:S(2)}) collective-permute-start(bf16[272,128]{1,0:T(8,128)(2,1)S(1)} %get-tuple-element.23), channel_id=1, source_target_pairs={{0,4},{1,5},{2,6},{3,7},{4,0},{5,1},{6,2},{7,3},{8,12},{9,13},{10,... | collective-permute-start | bytes 208904 | tf_op jit(solution)/shard_map/ppermute | solution.py:371
  44.5 1.9 %collective-permute-start.5 = (bf16[272,128]{1,0:T(8,128)(2,1)S(1)}, bf16[272,128]{1,0:T(8,128)(2,1)S(1)}, u32[]{:S(2)}, u32[]{:S(2)}) collective-permute-start(bf16[272,128]{1,0:T(8,128)(2,1)S(1)} %get-tuple-element.24), channel_id=1, source_target_pairs={{0,6},{1,7},{2,4},{3,5},{4,2},{5,3},{6,0},{7,1},{8,14},{9,15},{10,... | collective-permute-start | bytes 208904 | tf_op jit(solution)/shard_map/ppermute | solution.py:371
  46.5 4.3 %collective-permute-start.6 = (bf16[272,128]{1,0:T(8,128)(2,1)S(1)}, bf16[272,128]{1,0:T(8,128)(2,1)S(1)}, u32[]{:S(2)}, u32[]{:S(2)}) collective-permute-start(bf16[272,128]{1,0:T(8,128)(2,1)S(1)} %get-tuple-element.25), channel_id=1, source_target_pairs={{0,2},{1,3},{2,0},{3,1},{4,6},{5,7},{6,4},{7,5},{8,10},{9,11},{10,... | collective-permute-start | bytes 208904 | tf_op jit(solution)/shard_map/ppermute | solution.py:371
  50.8 0.0 collective-permute-done.4.in1
  50.8 5.5 %collective-permute-done.5.in2 = bf16[272,128]{1,0:T(8,128)(2,1)S(1)} collective-permute-done((bf16[272,128]{1,0:T(8,128)(2,1)S(1)}, bf16[272,128]{1,0:T(8,128)(2,1)S(1)}, u32[]{:S(2)}, u32[]{:S(2)}) %collective-permute-start.5) | collective-permute-done | bytes 69664 | tf_op jit(solution)/shard_map/ppermute | solution.py:371
  56.2 2.9 %collective-permute-done.6.in3 = bf16[272,128]{1,0:T(8,128)(2,1)S(1)} collective-permute-done((bf16[272,128]{1,0:T(8,128)(2,1)S(1)}, bf16[272,128]{1,0:T(8,128)(2,1)S(1)}, u32[]{:S(2)}, u32[]{:S(2)}) %collective-permute-start.6) | collective-permute-done | bytes 69664 | tf_op jit(solution)/shard_map/ppermute | solution.py:371
  59.2 0.0 copy-done.1
  59.2 1.2 %join_z.1 = (f32[32,256]{1,0:T(8,128)}, f32[32,256]{1,0:T(8,128)}, f32[1,128]{1,0:T(1,128)}) custom-call(bf16[272,128]{1,0:T(8,128)(2,1)S(1)} %get-tuple-element.22.in0, bf16[272,128]{1,0:T(8,128)(2,1)S(1)} %collective-permute-done.4.in1, bf16[272,128]{1,0:T(8,128)(2,1)S(1)} %collective-permute-done.5.in2, bf16[272,128]{1,0:T(8,128)(2,1)S(1)} %collective-permute-done.6.in3, ...), custom_call_target="tpu_custom_call" | custom-call | tf_op jit(solution)/shard_map/join_z/pallas_call | solution.py:307
Async XLA Ops:
  1.3 26.8 %copy-start = (f32[1024,2]{0,1:T(2,128)S(1)}, f32[1024,2]{0,1:T(2,128)}, u32[]{:S(2)}) copy-start(f32[1024,2]{0,1:T(2,128)} %param.15) | copy-start | bytes 24580
  6.9 52.3 %copy-start.1 = (f32[2]{0:T(128)S(1)}, f32[2]{0:T(128)}, u32[]{:S(2)}) copy-start(f32[2]{0:T(128)} %target_ref.1) | copy-start | bytes 28
  6.9 4.0 %collective-permute-start = (bf16[2704,128]{1,0:T(8,128)(2,1)S(1)}, bf16[2704,128]{1,0:T(8,128)(2,1)S(1)}, u32[]{:S(2)}, u32[]{:S(2)}) collective-permute-start(bf16[2704,128]{1,0:T(8,128)(2,1)S(1)} %get-tuple-element.17), channel_id=1, source_target_pairs={{0,1},{1,0},{2,3},{3,2},{4,5},{5,4},{6,7},{7,6},{8,9},{9,8},{10,11... | collective-permute-start | bytes 2076680 | tf_op jit(solution)/shard_map/ppermute | solution.py:368
  11.3 12.2 %collective-permute-start.1 = (bf16[912,128]{1,0:T(8,128)(2,1)S(1)}, bf16[912,128]{1,0:T(8,128)(2,1)S(1)}, u32[]{:S(2)}, u32[]{:S(2)}) collective-permute-start(bf16[912,128]{1,0:T(8,128)(2,1)S(1)} %get-tuple-element.19), channel_id=1, source_target_pairs={{0,16},{1,17},{2,18},{3,19},{4,20},{5,21},{6,22},{7,23},{8,24},{9,... | collective-permute-start | bytes 700424 | tf_op jit(solution)/shard_map/ppermute | solution.py:368
  16.4 11.2 %collective-permute-start.2 = (bf16[912,128]{1,0:T(8,128)(2,1)S(1)}, bf16[912,128]{1,0:T(8,128)(2,1)S(1)}, u32[]{:S(2)}, u32[]{:S(2)}) collective-permute-start(bf16[912,128]{1,0:T(8,128)(2,1)S(1)} %get-tuple-element.20), channel_id=1, source_target_pairs={{0,8},{1,9},{2,10},{3,11},{4,12},{5,13},{6,14},{7,15},{8,16},{9,17... | collective-permute-start | bytes 700424 | tf_op jit(solution)/shard_map/ppermute | solution.py:368
  19.0 9.1 %collective-permute-start.3 = (bf16[912,128]{1,0:T(8,128)(2,1)S(1)}, bf16[912,128]{1,0:T(8,128)(2,1)S(1)}, u32[]{:S(2)}, u32[]{:S(2)}) collective-permute-start(bf16[912,128]{1,0:T(8,128)(2,1)S(1)} %get-tuple-element.21), channel_id=1, source_target_pairs={{0,24},{1,25},{2,26},{3,27},{4,28},{5,29},{6,30},{7,31},{8,0},{9,1... | collective-permute-start | bytes 700424 | tf_op jit(solution)/shard_map/ppermute | solution.py:368
  28.8 22.0 %collective-permute-start.4 = (bf16[272,128]{1,0:T(8,128)(2,1)S(1)}, bf16[272,128]{1,0:T(8,128)(2,1)S(1)}, u32[]{:S(2)}, u32[]{:S(2)}) collective-permute-start(bf16[272,128]{1,0:T(8,128)(2,1)S(1)} %get-tuple-element.23), channel_id=1, source_target_pairs={{0,4},{1,5},{2,6},{3,7},{4,0},{5,1},{6,2},{7,3},{8,12},{9,13},{10,... | collective-permute-start | bytes 208904 | tf_op jit(solution)/shard_map/ppermute | solution.py:371
  44.5 11.7 %collective-permute-start.5 = (bf16[272,128]{1,0:T(8,128)(2,1)S(1)}, bf16[272,128]{1,0:T(8,128)(2,1)S(1)}, u32[]{:S(2)}, u32[]{:S(2)}) collective-permute-start(bf16[272,128]{1,0:T(8,128)(2,1)S(1)} %get-tuple-element.24), channel_id=1, source_target_pairs={{0,6},{1,7},{2,4},{3,5},{4,2},{5,3},{6,0},{7,1},{8,14},{9,15},{10,... | collective-permute-start | bytes 208904 | tf_op jit(solution)/shard_map/ppermute | solution.py:371
  46.5 12.7 %collective-permute-start.6 = (bf16[272,128]{1,0:T(8,128)(2,1)S(1)}, bf16[272,128]{1,0:T(8,128)(2,1)S(1)}, u32[]{:S(2)}, u32[]{:S(2)}) collective-permute-start(bf16[272,128]{1,0:T(8,128)(2,1)S(1)} %get-tuple-element.25), channel_id=1, source_target_pairs={{0,2},{1,3},{2,0},{3,1},{4,6},{5,7},{6,4},{7,5},{8,10},{9,11},{10,... | collective-permute-start | bytes 208904 | tf_op jit(solution)/shard_map/ppermute | solution.py:371

commit v5 on v4

--- a/solution.py
+++ b/solution.py
@@ -245,6 +245,9 @@
     return picked[:, 0:1] + picked[:, 1:2] + picked[:, 2:3]
 
 
+Z_AWAY = ((2, 3, 1), (2, 1, 3))
+
+
 def y_kernel(in0, in1, in2, in3, classifier_ref, *refs):
     in_refs, out_refs, w2_ref = (in0, in1, in2, in3), refs[:-1], refs[-1]
     notes = [read_note(r[Y_NOTE:, :], 5) for r in in_refs]
@@ -262,8 +265,9 @@
         sums.append(jnp.concatenate(halves, axis=1))
     w2_ref[...] = dot(jnp.concatenate(lefts, axis=1), jnp.concatenate(sums, axis=0), ((1,), (0,))).astype(BF16)
     here = lax.rem(lax.div(index, NC), NZ)
-    for away, out_ref in enumerate(out_refs):
-        z = lax.bitwise_xor(here, away)
+    odd = lax.rem(index, NC)
+    for even_away, odd_away, out_ref in zip((0, *Z_AWAY[0]), (0, *Z_AWAY[1]), out_refs):
+        z = lax.bitwise_xor(here, even_away + odd * (odd_away - even_away))
         part = pl.ds(pl.multiple_of(z * W1_PART, W1_PART), W1_PART)
         a, b = merge([r[part, :] for r in in_refs], shares, offsets)
         for i, block in enumerate((a, b)):
@@ -367,8 +371,8 @@
         ]
         return lax.ppermute(x, "tile", pairs)
 
-    def swap(x, dy, dz):
-        return lax.ppermute(x, "tile", [(place(y, z, c), place(y ^ dy, z ^ dz, c)) for y, z, c in everyone])
+    def swap(x, away):
+        return lax.ppermute(x, "tile", [(place(y, z, c), place(y, z ^ away[c], c)) for y, z, c in everyone])
 
     other = move(send, 0, 0, 1)
     piece = jax.ShapeDtypeStruct((Y_NOTE + NOTE, 128), BF16)
@@ -383,7 +387,7 @@
         "join_y",
         [pltpu.VMEM((2 * PATH_ROWS, hid), BF16)],
     )
-    across = [swap(pieces[2], 0, 2), swap(pieces[3], 0, 3), swap(pieces[1], 0, 1)]
+    across = [swap(pieces[k + 1], [away[k] for away in Z_AWAY]) for k in range(NZ - 1)]
     count = float(lax.axis_size("tile") * slots // 2)
     out = jax.ShapeDtypeStruct((ROWS, hid), F32)
     grad_w1, grad_w2, loss = call(

time: 61 us -> 59.7 us (0.979)
  waiting for transfers between devices: 15.2 us -> 13.6 us
    ppermute x3, waiting for transfers between devices: 8.39 us -> 6.8 us  [swap(): lax.ppermute(x, 'tile', [(place(y, z, c), place(y, z ^ away[c], c)) for y...]
where the time goes in v5:
time: 59.7 us; the launch traced here: 58.8 us
  starting transfers between devices  36 us (60%)
  waiting for transfers between devices  13.6 us (23%)
  Pallas kernels  7.81 us (13%)
  between operations  1.39 us (2%)
    ppermute x3, starting transfers between devices, swap(): lax.ppermute(x, 'tile', [(place(y, z, c), place(y, z ^ away[c], c)) for y...  21.9 us
    ppermute x4, starting transfers between devices, move(): return lax.ppermute(x, 'tile', pairs)  14.1 us
    pallas_call x4, Pallas kernels, call(): pl.pallas_call(kernel, out_shape=out_shape, in_specs=in_specs, out_specs=...  7.81 us
    ppermute x3, waiting for transfers between devices, swap(): lax.ppermute(x, 'tile', [(place(y, z, c), place(y, z ^ away[c], c)) for y...  6.8 us
    ppermute x4, waiting for transfers between devices, move(): return lax.ppermute(x, 'tile', pairs)  6.78 us
  transfers between devices with their start and end apart: 7, of which 5 were waited for; matrix products, arithmetic and copies ran while one was open for 0% of the time, Pallas kernels for 0%

profile of v5, /device:TPU:6, one launch (start us, length us, event | category | flops | bytes accessed | tf_op | source)
XLA Modules:
  0.0 58.8 jit_solution(6833372502963622913)
XLA Ops:
  1.3 0.0 copy-start
  1.3 5.6 %local.1 = (bf16[2704,128]{1,0:T(8,128)(2,1)S(1)}, bf16[2704,128]{1,0:T(8,128)(2,1)S(1)}) custom-call(s32[1]{0:T(128)S(6)} %copy.12.count_ref, bf16[1024,1024]{1,0:T(8,128)(2,1)} %bitcast.7, bf16[1024,256]{1,0:T(8,128)(2,1)} %w_reduce_hbm.1, bf16[1024,256]{1,0:T(8,128)(2,1)} %w_expand_hbm.1, bf16[1024,256]{1,0:T(8,128)(2,1)} %att_tanh_hbm.1, ...), custom_call_target="tpu_custom_call" | custom-call | tf_op jit(solution)/shard_map/local/pallas_call | solution.py:311
  6.9 0.0 copy-start.1
  6.9 1.9 %collective-permute-start = (bf16[2704,128]{1,0:T(8,128)(2,1)S(1)}, bf16[2704,128]{1,0:T(8,128)(2,1)S(1)}, u32[]{:S(2)}, u32[]{:S(2)}) collective-permute-start(bf16[2704,128]{1,0:T(8,128)(2,1)S(1)} %get-tuple-element.17), channel_id=1, source_target_pairs={{0,1},{1,0},{2,3},{3,2},{4,5},{5,4},{6,7},{7,6},{8,9},{9,8},{10,11... | collective-permute-start | bytes 2076680 | tf_op jit(solution)/shard_map/ppermute | solution.py:372
  8.8 2.1 %collective-permute-done.other_ref = bf16[2704,128]{1,0:T(8,128)(2,1)S(1)} collective-permute-done((bf16[2704,128]{1,0:T(8,128)(2,1)S(1)}, bf16[2704,128]{1,0:T(8,128)(2,1)S(1)}, u32[]{:S(2)}, u32[]{:S(2)}) %collective-permute-start) | collective-permute-done | bytes 692256 | tf_op jit(solution)/shard_map/ppermute | solution.py:372
  11.0 0.3 join_cores.1
  11.3 5.1 %collective-permute-start.1 = (bf16[912,128]{1,0:T(8,128)(2,1)S(1)}, bf16[912,128]{1,0:T(8,128)(2,1)S(1)}, u32[]{:S(2)}, u32[]{:S(2)}) collective-permute-start(bf16[912,128]{1,0:T(8,128)(2,1)S(1)} %get-tuple-element.19), channel_id=1, source_target_pairs={{0,16},{1,17},{2,18},{3,19},{4,20},{5,21},{6,22},{7,23},{8,24},{9,... | collective-permute-start | bytes 700424 | tf_op jit(solution)/shard_map/ppermute | solution.py:372
  16.4 2.6 %collective-permute-start.2 = (bf16[912,128]{1,0:T(8,128)(2,1)S(1)}, bf16[912,128]{1,0:T(8,128)(2,1)S(1)}, u32[]{:S(2)}, u32[]{:S(2)}) collective-permute-start(bf16[912,128]{1,0:T(8,128)(2,1)S(1)} %get-tuple-element.20), channel_id=1, source_target_pairs={{0,8},{1,9},{2,10},{3,11},{4,12},{5,13},{6,14},{7,15},{8,16},{9,17... | collective-permute-start | bytes 700424 | tf_op jit(solution)/shard_map/ppermute | solution.py:372
  19.0 4.5 %collective-permute-start.3 = (bf16[912,128]{1,0:T(8,128)(2,1)S(1)}, bf16[912,128]{1,0:T(8,128)(2,1)S(1)}, u32[]{:S(2)}, u32[]{:S(2)}) collective-permute-start(bf16[912,128]{1,0:T(8,128)(2,1)S(1)} %get-tuple-element.21), channel_id=1, source_target_pairs={{0,24},{1,25},{2,26},{3,27},{4,28},{5,29},{6,30},{7,31},{8,0},{9,1... | collective-permute-start | bytes 700424 | tf_op jit(solution)/shard_map/ppermute | solution.py:372
  23.4 0.0 collective-permute-done.1.in1
  23.5 4.1 %collective-permute-done.2.in2 = bf16[912,128]{1,0:T(8,128)(2,1)S(1)} collective-permute-done((bf16[912,128]{1,0:T(8,128)(2,1)S(1)}, bf16[912,128]{1,0:T(8,128)(2,1)S(1)}, u32[]{:S(2)}, u32[]{:S(2)}) %collective-permute-start.2) | collective-permute-done | bytes 233504 | tf_op jit(solution)/shard_map/ppermute | solution.py:372
  27.6 0.5 collective-permute-done.3.in3
  28.1 0.0 copy-done
  28.1 0.7 %join_y.1 = (bf16[272,128]{1,0:T(8,128)(2,1)S(1)}, bf16[272,128]{1,0:T(8,128)(2,1)S(1)}, bf16[272,128]{1,0:T(8,128)(2,1)S(1)}, bf16[272,128]{1,0:T(8,128)(2,1)S(1)}) custom-call(bf16[912,128]{1,0:T(8,128)(2,1)S(1)} %get-tuple-element.18.in0, bf16[912,128]{1,0:T(8,128)(2,1)S(1)} %collective-permute-done.1.in1, ...), custom_call_target="tpu_custom_call" | custom-call | tf_op jit(solution)/shard_map/join_y/pallas_call | solution.py:311
  28.8 15.7 %collective-permute-start.4 = (bf16[272,128]{1,0:T(8,128)(2,1)S(1)}, bf16[272,128]{1,0:T(8,128)(2,1)S(1)}, u32[]{:S(2)}, u32[]{:S(2)}) collective-permute-start(bf16[272,128]{1,0:T(8,128)(2,1)S(1)} %get-tuple-element.23), channel_id=1, source_target_pairs={{0,4},{1,5},{2,6},{3,7},{4,0},{5,1},{6,2},{7,3},{8,12},{9,13},{10,... | collective-permute-start | bytes 208904 | tf_op jit(solution)/shard_map/ppermute | solution.py:375
  44.5 1.9 %collective-permute-start.5 = (bf16[272,128]{1,0:T(8,128)(2,1)S(1)}, bf16[272,128]{1,0:T(8,128)(2,1)S(1)}, u32[]{:S(2)}, u32[]{:S(2)}) collective-permute-start(bf16[272,128]{1,0:T(8,128)(2,1)S(1)} %get-tuple-element.24), channel_id=1, source_target_pairs={{0,6},{1,3},{2,4},{3,1},{4,2},{5,7},{6,0},{7,5},{8,14},{9,11},{10,... | collective-permute-start | bytes 208904 | tf_op jit(solution)/shard_map/ppermute | solution.py:375
  46.5 4.3 %collective-permute-start.6 = (bf16[272,128]{1,0:T(8,128)(2,1)S(1)}, bf16[272,128]{1,0:T(8,128)(2,1)S(1)}, u32[]{:S(2)}, u32[]{:S(2)}) collective-permute-start(bf16[272,128]{1,0:T(8,128)(2,1)S(1)} %get-tuple-element.25), channel_id=1, source_target_pairs={{0,2},{1,7},{2,0},{3,5},{4,6},{5,3},{6,4},{7,1},{8,10},{9,15},{10,... | collective-permute-start | bytes 208904 | tf_op jit(solution)/shard_map/ppermute | solution.py:375
  50.8 0.0 collective-permute-done.4.in1
  50.8 5.5 %collective-permute-done.5.in2 = bf16[272,128]{1,0:T(8,128)(2,1)S(1)} collective-permute-done((bf16[272,128]{1,0:T(8,128)(2,1)S(1)}, bf16[272,128]{1,0:T(8,128)(2,1)S(1)}, u32[]{:S(2)}, u32[]{:S(2)}) %collective-permute-start.5) | collective-permute-done | bytes 69664 | tf_op jit(solution)/shard_map/ppermute | solution.py:375
  56.3 1.3 %collective-permute-done.6.in3 = bf16[272,128]{1,0:T(8,128)(2,1)S(1)} collective-permute-done((bf16[272,128]{1,0:T(8,128)(2,1)S(1)}, bf16[272,128]{1,0:T(8,128)(2,1)S(1)}, u32[]{:S(2)}, u32[]{:S(2)}) %collective-permute-start.6) | collective-permute-done | bytes 69664 | tf_op jit(solution)/shard_map/ppermute | solution.py:375
  57.6 0.0 copy-done.1
  57.6 1.2 %join_z.1 = (f32[32,256]{1,0:T(8,128)}, f32[32,256]{1,0:T(8,128)}, f32[1,128]{1,0:T(1,128)}) custom-call(bf16[272,128]{1,0:T(8,128)(2,1)S(1)} %get-tuple-element.22.in0, bf16[272,128]{1,0:T(8,128)(2,1)S(1)} %collective-permute-done.4.in1, bf16[272,128]{1,0:T(8,128)(2,1)S(1)} %collective-permute-done.5.in2, bf16[272,128]{1,0:T(8,128)(2,1)S(1)} %collective-permute-done.6.in3, ...), custom_call_target="tpu_custom_call" | custom-call | tf_op jit(solution)/shard_map/join_z/pallas_call | solution.py:311
Async XLA Ops:
  1.3 26.8 %copy-start = (f32[1024,2]{0,1:T(2,128)S(1)}, f32[1024,2]{0,1:T(2,128)}, u32[]{:S(2)}) copy-start(f32[1024,2]{0,1:T(2,128)} %param.15) | copy-start | bytes 24580
  6.9 50.7 %copy-start.1 = (f32[2]{0:T(128)S(1)}, f32[2]{0:T(128)}, u32[]{:S(2)}) copy-start(f32[2]{0:T(128)} %target_ref.1) | copy-start | bytes 28
  6.9 4.0 %collective-permute-start = (bf16[2704,128]{1,0:T(8,128)(2,1)S(1)}, bf16[2704,128]{1,0:T(8,128)(2,1)S(1)}, u32[]{:S(2)}, u32[]{:S(2)}) collective-permute-start(bf16[2704,128]{1,0:T(8,128)(2,1)S(1)} %get-tuple-element.17), channel_id=1, source_target_pairs={{0,1},{1,0},{2,3},{3,2},{4,5},{5,4},{6,7},{7,6},{8,9},{9,8},{10,11... | collective-permute-start | bytes 2076680 | tf_op jit(solution)/shard_map/ppermute | solution.py:372
  11.3 12.2 %collective-permute-start.1 = (bf16[912,128]{1,0:T(8,128)(2,1)S(1)}, bf16[912,128]{1,0:T(8,128)(2,1)S(1)}, u32[]{:S(2)}, u32[]{:S(2)}) collective-permute-start(bf16[912,128]{1,0:T(8,128)(2,1)S(1)} %get-tuple-element.19), channel_id=1, source_target_pairs={{0,16},{1,17},{2,18},{3,19},{4,20},{5,21},{6,22},{7,23},{8,24},{9,... | collective-permute-start | bytes 700424 | tf_op jit(solution)/shard_map/ppermute | solution.py:372
  16.4 11.2 %collective-permute-start.2 = (bf16[912,128]{1,0:T(8,128)(2,1)S(1)}, bf16[912,128]{1,0:T(8,128)(2,1)S(1)}, u32[]{:S(2)}, u32[]{:S(2)}) collective-permute-start(bf16[912,128]{1,0:T(8,128)(2,1)S(1)} %get-tuple-element.20), channel_id=1, source_target_pairs={{0,8},{1,9},{2,10},{3,11},{4,12},{5,13},{6,14},{7,15},{8,16},{9,17... | collective-permute-start | bytes 700424 | tf_op jit(solution)/shard_map/ppermute | solution.py:372
  19.0 9.1 %collective-permute-start.3 = (bf16[912,128]{1,0:T(8,128)(2,1)S(1)}, bf16[912,128]{1,0:T(8,128)(2,1)S(1)}, u32[]{:S(2)}, u32[]{:S(2)}) collective-permute-start(bf16[912,128]{1,0:T(8,128)(2,1)S(1)} %get-tuple-element.21), channel_id=1, source_target_pairs={{0,24},{1,25},{2,26},{3,27},{4,28},{5,29},{6,30},{7,31},{8,0},{9,1... | collective-permute-start | bytes 700424 | tf_op jit(solution)/shard_map/ppermute | solution.py:372
  28.8 22.0 %collective-permute-start.4 = (bf16[272,128]{1,0:T(8,128)(2,1)S(1)}, bf16[272,128]{1,0:T(8,128)(2,1)S(1)}, u32[]{:S(2)}, u32[]{:S(2)}) collective-permute-start(bf16[272,128]{1,0:T(8,128)(2,1)S(1)} %get-tuple-element.23), channel_id=1, source_target_pairs={{0,4},{1,5},{2,6},{3,7},{4,0},{5,1},{6,2},{7,3},{8,12},{9,13},{10,... | collective-permute-start | bytes 208904 | tf_op jit(solution)/shard_map/ppermute | solution.py:375
  44.5 11.8 %collective-permute-start.5 = (bf16[272,128]{1,0:T(8,128)(2,1)S(1)}, bf16[272,128]{1,0:T(8,128)(2,1)S(1)}, u32[]{:S(2)}, u32[]{:S(2)}) collective-permute-start(bf16[272,128]{1,0:T(8,128)(2,1)S(1)} %get-tuple-element.24), channel_id=1, source_target_pairs={{0,6},{1,3},{2,4},{3,1},{4,2},{5,7},{6,0},{7,5},{8,14},{9,11},{10,... | collective-permute-start | bytes 208904 | tf_op jit(solution)/shard_map/ppermute | solution.py:375
  46.5 11.1 %collective-permute-start.6 = (bf16[272,128]{1,0:T(8,128)(2,1)S(1)}, bf16[272,128]{1,0:T(8,128)(2,1)S(1)}, u32[]{:S(2)}, u32[]{:S(2)}) collective-permute-start(bf16[272,128]{1,0:T(8,128)(2,1)S(1)} %get-tuple-element.25), channel_id=1, source_target_pairs={{0,2},{1,7},{2,0},{3,5},{4,6},{5,3},{6,4},{7,1},{8,10},{9,15},{10,... | collective-permute-start | bytes 208904 | tf_op jit(solution)/shard_map/ppermute | solution.py:375

commit v6 on v5

--- a/solution.py
+++ b/solution.py
@@ -82,12 +82,13 @@
 
 def store_path(path, keep_ref, send_ref):
     first = lax.rem(lax.axis_index("tile"), NC) == 0
+    own = lax.broadcasted_iota(jnp.int32, (ROWS, 2 * SLOTS), 1) < SLOTS
     for k in range(NY * NZ):
         at = k * NC * ROWS
         even, odd = path[at : at + ROWS], path[at + ROWS : at + 2 * ROWS]
         here = pl.ds(CORE_PATH + k * ROWS, ROWS)
-        keep_ref[here, :] = jnp.where(first, even[:, :128], odd[:, :128]).astype(BF16)
-        send_ref[here, :] = jnp.where(first, odd[:, 128:], even[:, 128:]).astype(BF16)
+        keep_ref[here, :] = jnp.where(own, jnp.where(first, even, odd), 0.0).astype(BF16)
+        send_ref[here, :] = jnp.where(own, 0.0, jnp.where(first, odd, even)).astype(BF16)
 
 
 def as_row(column, shift):
@@ -177,9 +178,8 @@
     path = dot(e_tanh, att_tanh, ((1,), (1,))) + dot(e_gate, att_gate, ((1,), (1,)))
     dy_a = ((share * (class0 - class1) + slope * path) * (1.0 / 16.0)).astype(BF16)
     dy_b = (share * path * (1.0 / 16.0)).astype(BF16)
-    blank = jnp.zeros((2 * slots, e_tanh.shape[1]), BF16)
-    path_t = dot(att_tanh, jnp.concatenate([e_tanh, blank, e_tanh], axis=0), ((1,), (1,))) + dot(
-        att_gate, jnp.concatenate([e_gate, blank, e_gate], axis=0), ((1,), (1,))
+    path_t = dot(att_tanh, jnp.concatenate([e_tanh, e_tanh], axis=0), ((1,), (1,))) + dot(
+        att_gate, jnp.concatenate([e_gate, e_gate], axis=0), ((1,), (1,))
     )
     store_path(path_t, keep_ref, send_ref)
     scalars = [jnp.broadcast_to(v, (1, 128)) for v in (total, mean0, mean1)]

time: 59.7 us -> 59.7 us (level)
  no operation moved by 1% of the time
where the time goes in v6:
time: 59.7 us; the launch traced here: 58.8 us
  starting transfers between devices  36 us (60%)
  waiting for transfers between devices  13.6 us (23%)
  Pallas kernels  7.78 us (13%)
  between operations  1.39 us (2%)
    ppermute x3, starting transfers between devices, swap(): lax.ppermute(x, 'tile', [(place(y, z, c), place(y, z ^ away[c], c)) for y...  21.9 us
    ppermute x4, starting transfers between devices, move(): return lax.ppermute(x, 'tile', pairs)  14.1 us
    pallas_call x4, Pallas kernels, call(): pl.pallas_call(kernel, out_shape=out_shape, in_specs=in_specs, out_specs=...  7.78 us
    ppermute x3, waiting for transfers between devices, swap(): lax.ppermute(x, 'tile', [(place(y, z, c), place(y, z ^ away[c], c)) for y...  6.8 us
    ppermute x4, waiting for transfers between devices, move(): return lax.ppermute(x, 'tile', pairs)  6.78 us
  transfers between devices with their start and end apart: 7, of which 5 were waited for; matrix products, arithmetic and copies ran while one was open for 0% of the time, Pallas kernels for 0%

profile of v6, /device:TPU:6, one launch (start us, length us, event | category | flops | bytes accessed | tf_op | source)
XLA Modules:
  0.0 58.8 jit_solution(7109130693733569595)
XLA Ops:
  1.3 0.0 copy-start
  1.3 5.6 %local.1 = (bf16[2704,128]{1,0:T(8,128)(2,1)S(1)}, bf16[2704,128]{1,0:T(8,128)(2,1)S(1)}) custom-call(s32[1]{0:T(128)S(6)} %copy.12.count_ref, bf16[1024,1024]{1,0:T(8,128)(2,1)} %bitcast.7, bf16[1024,256]{1,0:T(8,128)(2,1)} %w_reduce_hbm.1, bf16[1024,256]{1,0:T(8,128)(2,1)} %w_expand_hbm.1, bf16[1024,256]{1,0:T(8,128)(2,1)} %att_tanh_hbm.1, ...), custom_call_target="tpu_custom_call" | custom-call | tf_op jit(solution)/shard_map/local/pallas_call | solution.py:311
  6.9 0.0 copy-start.1
  6.9 1.9 %collective-permute-start = (bf16[2704,128]{1,0:T(8,128)(2,1)S(1)}, bf16[2704,128]{1,0:T(8,128)(2,1)S(1)}, u32[]{:S(2)}, u32[]{:S(2)}) collective-permute-start(bf16[2704,128]{1,0:T(8,128)(2,1)S(1)} %get-tuple-element.17), channel_id=1, source_target_pairs={{0,1},{1,0},{2,3},{3,2},{4,5},{5,4},{6,7},{7,6},{8,9},{9,8},{10,11... | collective-permute-start | bytes 2076680 | tf_op jit(solution)/shard_map/ppermute | solution.py:372
  8.8 2.1 %collective-permute-done.other_ref = bf16[2704,128]{1,0:T(8,128)(2,1)S(1)} collective-permute-done((bf16[2704,128]{1,0:T(8,128)(2,1)S(1)}, bf16[2704,128]{1,0:T(8,128)(2,1)S(1)}, u32[]{:S(2)}, u32[]{:S(2)}) %collective-permute-start) | collective-permute-done | bytes 692256 | tf_op jit(solution)/shard_map/ppermute | solution.py:372
  10.9 0.3 join_cores.1
  11.2 5.1 %collective-permute-start.1 = (bf16[912,128]{1,0:T(8,128)(2,1)S(1)}, bf16[912,128]{1,0:T(8,128)(2,1)S(1)}, u32[]{:S(2)}, u32[]{:S(2)}) collective-permute-start(bf16[912,128]{1,0:T(8,128)(2,1)S(1)} %get-tuple-element.19), channel_id=1, source_target_pairs={{0,16},{1,17},{2,18},{3,19},{4,20},{5,21},{6,22},{7,23},{8,24},{9,... | collective-permute-start | bytes 700424 | tf_op jit(solution)/shard_map/ppermute | solution.py:372
  16.3 2.6 %collective-permute-start.2 = (bf16[912,128]{1,0:T(8,128)(2,1)S(1)}, bf16[912,128]{1,0:T(8,128)(2,1)S(1)}, u32[]{:S(2)}, u32[]{:S(2)}) collective-permute-start(bf16[912,128]{1,0:T(8,128)(2,1)S(1)} %get-tuple-element.20), channel_id=1, source_target_pairs={{0,8},{1,9},{2,10},{3,11},{4,12},{5,13},{6,14},{7,15},{8,16},{9,17... | collective-permute-start | bytes 700424 | tf_op jit(solution)/shard_map/ppermute | solution.py:372
  18.9 4.5 %collective-permute-start.3 = (bf16[912,128]{1,0:T(8,128)(2,1)S(1)}, bf16[912,128]{1,0:T(8,128)(2,1)S(1)}, u32[]{:S(2)}, u32[]{:S(2)}) collective-permute-start(bf16[912,128]{1,0:T(8,128)(2,1)S(1)} %get-tuple-element.21), channel_id=1, source_target_pairs={{0,24},{1,25},{2,26},{3,27},{4,28},{5,29},{6,30},{7,31},{8,0},{9,1... | collective-permute-start | bytes 700424 | tf_op jit(solution)/shard_map/ppermute | solution.py:372
  23.4 0.0 collective-permute-done.1.in1
  23.4 4.1 %collective-permute-done.2.in2 = bf16[912,128]{1,0:T(8,128)(2,1)S(1)} collective-permute-done((bf16[912,128]{1,0:T(8,128)(2,1)S(1)}, bf16[912,128]{1,0:T(8,128)(2,1)S(1)}, u32[]{:S(2)}, u32[]{:S(2)}) %collective-permute-start.2) | collective-permute-done | bytes 233504 | tf_op jit(solution)/shard_map/ppermute | solution.py:372
  27.5 0.5 collective-permute-done.3.in3
  28.1 0.0 copy-done
  28.1 0.7 %join_y.1 = (bf16[272,128]{1,0:T(8,128)(2,1)S(1)}, bf16[272,128]{1,0:T(8,128)(2,1)S(1)}, bf16[272,128]{1,0:T(8,128)(2,1)S(1)}, bf16[272,128]{1,0:T(8,128)(2,1)S(1)}) custom-call(bf16[912,128]{1,0:T(8,128)(2,1)S(1)} %get-tuple-element.18.in0, bf16[912,128]{1,0:T(8,128)(2,1)S(1)} %collective-permute-done.1.in1, ...), custom_call_target="tpu_custom_call" | custom-call | tf_op jit(solution)/shard_map/join_y/pallas_call | solution.py:311
  28.8 15.7 %collective-permute-start.4 = (bf16[272,128]{1,0:T(8,128)(2,1)S(1)}, bf16[272,128]{1,0:T(8,128)(2,1)S(1)}, u32[]{:S(2)}, u32[]{:S(2)}) collective-permute-start(bf16[272,128]{1,0:T(8,128)(2,1)S(1)} %get-tuple-element.23), channel_id=1, source_target_pairs={{0,4},{1,5},{2,6},{3,7},{4,0},{5,1},{6,2},{7,3},{8,12},{9,13},{10,... | collective-permute-start | bytes 208904 | tf_op jit(solution)/shard_map/ppermute | solution.py:375
  44.5 1.9 %collective-permute-start.5 = (bf16[272,128]{1,0:T(8,128)(2,1)S(1)}, bf16[272,128]{1,0:T(8,128)(2,1)S(1)}, u32[]{:S(2)}, u32[]{:S(2)}) collective-permute-start(bf16[272,128]{1,0:T(8,128)(2,1)S(1)} %get-tuple-element.24), channel_id=1, source_target_pairs={{0,6},{1,3},{2,4},{3,1},{4,2},{5,7},{6,0},{7,5},{8,14},{9,11},{10,... | collective-permute-start | bytes 208904 | tf_op jit(solution)/shard_map/ppermute | solution.py:375
  46.4 4.3 %collective-permute-start.6 = (bf16[272,128]{1,0:T(8,128)(2,1)S(1)}, bf16[272,128]{1,0:T(8,128)(2,1)S(1)}, u32[]{:S(2)}, u32[]{:S(2)}) collective-permute-start(bf16[272,128]{1,0:T(8,128)(2,1)S(1)} %get-tuple-element.25), channel_id=1, source_target_pairs={{0,2},{1,7},{2,0},{3,5},{4,6},{5,3},{6,4},{7,1},{8,10},{9,15},{10,... | collective-permute-start | bytes 208904 | tf_op jit(solution)/shard_map/ppermute | solution.py:375
  50.7 0.0 collective-permute-done.4.in1
  50.7 5.5 %collective-permute-done.5.in2 = bf16[272,128]{1,0:T(8,128)(2,1)S(1)} collective-permute-done((bf16[272,128]{1,0:T(8,128)(2,1)S(1)}, bf16[272,128]{1,0:T(8,128)(2,1)S(1)}, u32[]{:S(2)}, u32[]{:S(2)}) %collective-permute-start.5) | collective-permute-done | bytes 69664 | tf_op jit(solution)/shard_map/ppermute | solution.py:375
  56.3 1.3 %collective-permute-done.6.in3 = bf16[272,128]{1,0:T(8,128)(2,1)S(1)} collective-permute-done((bf16[272,128]{1,0:T(8,128)(2,1)S(1)}, bf16[272,128]{1,0:T(8,128)(2,1)S(1)}, u32[]{:S(2)}, u32[]{:S(2)}) %collective-permute-start.6) | collective-permute-done | bytes 69664 | tf_op jit(solution)/shard_map/ppermute | solution.py:375
  57.5 0.0 copy-done.1
  57.5 1.2 %join_z.1 = (f32[32,256]{1,0:T(8,128)}, f32[32,256]{1,0:T(8,128)}, f32[1,128]{1,0:T(1,128)}) custom-call(bf16[272,128]{1,0:T(8,128)(2,1)S(1)} %get-tuple-element.22.in0, bf16[272,128]{1,0:T(8,128)(2,1)S(1)} %collective-permute-done.4.in1, bf16[272,128]{1,0:T(8,128)(2,1)S(1)} %collective-permute-done.5.in2, bf16[272,128]{1,0:T(8,128)(2,1)S(1)} %collective-permute-done.6.in3, ...), custom_call_target="tpu_custom_call" | custom-call | tf_op jit(solution)/shard_map/join_z/pallas_call | solution.py:311
Async XLA Ops:
  1.3 26.8 %copy-start = (f32[1024,2]{0,1:T(2,128)S(1)}, f32[1024,2]{0,1:T(2,128)}, u32[]{:S(2)}) copy-start(f32[1024,2]{0,1:T(2,128)} %param.15) | copy-start | bytes 24580
  6.9 50.7 %copy-start.1 = (f32[2]{0:T(128)S(1)}, f32[2]{0:T(128)}, u32[]{:S(2)}) copy-start(f32[2]{0:T(128)} %target_ref.1) | copy-start | bytes 28
  6.9 4.0 %collective-permute-start = (bf16[2704,128]{1,0:T(8,128)(2,1)S(1)}, bf16[2704,128]{1,0:T(8,128)(2,1)S(1)}, u32[]{:S(2)}, u32[]{:S(2)}) collective-permute-start(bf16[2704,128]{1,0:T(8,128)(2,1)S(1)} %get-tuple-element.17), channel_id=1, source_target_pairs={{0,1},{1,0},{2,3},{3,2},{4,5},{5,4},{6,7},{7,6},{8,9},{9,8},{10,11... | collective-permute-start | bytes 2076680 | tf_op jit(solution)/shard_map/ppermute | solution.py:372
  11.2 12.2 %collective-permute-start.1 = (bf16[912,128]{1,0:T(8,128)(2,1)S(1)}, bf16[912,128]{1,0:T(8,128)(2,1)S(1)}, u32[]{:S(2)}, u32[]{:S(2)}) collective-permute-start(bf16[912,128]{1,0:T(8,128)(2,1)S(1)} %get-tuple-element.19), channel_id=1, source_target_pairs={{0,16},{1,17},{2,18},{3,19},{4,20},{5,21},{6,22},{7,23},{8,24},{9,... | collective-permute-start | bytes 700424 | tf_op jit(solution)/shard_map/ppermute | solution.py:372
  16.3 11.2 %collective-permute-start.2 = (bf16[912,128]{1,0:T(8,128)(2,1)S(1)}, bf16[912,128]{1,0:T(8,128)(2,1)S(1)}, u32[]{:S(2)}, u32[]{:S(2)}) collective-permute-start(bf16[912,128]{1,0:T(8,128)(2,1)S(1)} %get-tuple-element.20), channel_id=1, source_target_pairs={{0,8},{1,9},{2,10},{3,11},{4,12},{5,13},{6,14},{7,15},{8,16},{9,17... | collective-permute-start | bytes 700424 | tf_op jit(solution)/shard_map/ppermute | solution.py:372
  18.9 9.1 %collective-permute-start.3 = (bf16[912,128]{1,0:T(8,128)(2,1)S(1)}, bf16[912,128]{1,0:T(8,128)(2,1)S(1)}, u32[]{:S(2)}, u32[]{:S(2)}) collective-permute-start(bf16[912,128]{1,0:T(8,128)(2,1)S(1)} %get-tuple-element.21), channel_id=1, source_target_pairs={{0,24},{1,25},{2,26},{3,27},{4,28},{5,29},{6,30},{7,31},{8,0},{9,1... | collective-permute-start | bytes 700424 | tf_op jit(solution)/shard_map/ppermute | solution.py:372
  28.8 22.0 %collective-permute-start.4 = (bf16[272,128]{1,0:T(8,128)(2,1)S(1)}, bf16[272,128]{1,0:T(8,128)(2,1)S(1)}, u32[]{:S(2)}, u32[]{:S(2)}) collective-permute-start(bf16[272,128]{1,0:T(8,128)(2,1)S(1)} %get-tuple-element.23), channel_id=1, source_target_pairs={{0,4},{1,5},{2,6},{3,7},{4,0},{5,1},{6,2},{7,3},{8,12},{9,13},{10,... | collective-permute-start | bytes 208904 | tf_op jit(solution)/shard_map/ppermute | solution.py:375
  44.5 11.8 %collective-permute-start.5 = (bf16[272,128]{1,0:T(8,128)(2,1)S(1)}, bf16[272,128]{1,0:T(8,128)(2,1)S(1)}, u32[]{:S(2)}, u32[]{:S(2)}) collective-permute-start(bf16[272,128]{1,0:T(8,128)(2,1)S(1)} %get-tuple-element.24), channel_id=1, source_target_pairs={{0,6},{1,3},{2,4},{3,1},{4,2},{5,7},{6,0},{7,5},{8,14},{9,11},{10,... | collective-permute-start | bytes 208904 | tf_op jit(solution)/shard_map/ppermute | solution.py:375
  46.4 11.1 %collective-permute-start.6 = (bf16[272,128]{1,0:T(8,128)(2,1)S(1)}, bf16[272,128]{1,0:T(8,128)(2,1)S(1)}, u32[]{:S(2)}, u32[]{:S(2)}) collective-permute-start(bf16[272,128]{1,0:T(8,128)(2,1)S(1)} %get-tuple-element.25), channel_id=1, source_target_pairs={{0,2},{1,7},{2,0},{3,5},{4,6},{5,3},{6,4},{7,1},{8,10},{9,15},{10,... | collective-permute-start | bytes 208904 | tf_op jit(solution)/shard_map/ppermute | solution.py:375
